TPU v7x, 128 devices: a whole 4x4x4 slice. The times are simulated.
128 devices in a mesh: cell: 16 (over y, x), gene: 8 (over z, core).
Axes of the slice: x: 4, y: 4, z: 4, core: 2. Of those that a mesh axis runs over, the one named last changes fastest.
Arguments:
- expression: float32 [24576, 32768], P('cell', 'gene'), may hold values from -16 to 18, as said below
- tile_mask: int32 [96, 128], P('cell', 'gene'), may hold values from 0 to 1, as said below
- start: float32 [32768, 32], P('gene'), may hold values from -6 to 6
Outputs:
- alphas: float32 [2, 32, 32], replicated
- betas: float32 [2, 32, 32], replicated
- next_block: float32 [32768, 32], P('gene')
Inputs may be any that keep to these rules, and one draw needn't show every extreme that they name: expression: positive mean per gene with gene and cell scales and independent noise. `tile_mask`: each row of tiles belongs to one of 8 cell types and each column of tiles to one of 8 gene modules; a tile is 1 where its type expresses its module.
All inputs are finite; a program needn't handle non-finite values.
Results may differ from a plain program's by a relative error of at most 0.0024.
Values sent between devices are 32-bit elements; how exact they have to be, the bound alone decides.
A program may use at most 128 MiB of HBM per device.

v0:
```python
import math

import jax
import jax.numpy as jnp
from jax import lax
from jax.sharding import PartitionSpec as P

TILE = 256
STEPS = 2


highest = lax.Precision.HIGHEST


def transposed_dot(left, right):
    return lax.dot_general(
        left, right, (((0,), (0,)), ((), ())), precision=highest, preferred_element_type=jnp.float32
    )


def product(left, right):
    return jnp.dot(left, right, precision=highest, preferred_element_type=jnp.float32)


def finish(resid, gram):
    lower = jnp.linalg.cholesky(gram)
    fresh = lax.linalg.triangular_solve(lower, resid, left_side=False, lower=True, transpose_a=True)
    return (fresh, jnp.transpose(lower))


def expand_mask(expression, tile_mask):
    rows, width = expression.shape
    tiles = expression.reshape(tile_mask.shape[0], TILE, tile_mask.shape[1], TILE)
    return (tiles * tile_mask.astype(jnp.float32)[:, None, :, None]).reshape(rows, width)


def orthogonalize(image, current, older):
    projections = [transposed_dot(current, image)]
    if older is not None:
        projections.append(transposed_dot(older, image))
    summed = lax.psum(jnp.stack(projections), "gene")
    resid = image - product(current, summed[0])
    if older is not None:
        resid = resid - product(older, summed[1])
    gram = lax.psum(transposed_dot(resid, resid), "gene")
    fresh, beta = finish(resid, gram)
    return (fresh, summed[0], beta)


def per_device(expression, tile_mask, start):
    cell_count = lax.axis_size("cell")
    gene_count = lax.axis_size("gene")
    rows, width = expression.shape
    cells = rows * cell_count
    masked = expand_mask(expression, tile_mask)
    means = lax.psum(jnp.sum(masked, axis=0), "cell") / cells
    current = start
    gram_start = lax.psum(transposed_dot(current, current), "gene")
    current = finish(current, gram_start)[0]
    older = None
    alpha_list = []
    beta_list = []
    for step in range(STEPS):
        partial_side = product(masked, current) - product(means[None, :], current)
        cell_side = lax.psum(partial_side, "gene")
        image = lax.psum(transposed_dot(masked, cell_side) / cells, "cell")
        fresh, alpha, beta = orthogonalize(image, current, older)
        alpha_list.append(alpha)
        beta_list.append(beta)
        older = current
        current = fresh
    next_block = current * math.sqrt(width * gene_count)
    return (jnp.stack(alpha_list), jnp.stack(beta_list), next_block)


def solution(mesh):
    in_specs = (P("cell", "gene"), P("cell", "gene"), P("gene", None))
    out_specs = (P(), P(), P("gene", None))
    return jax.shard_map(
        per_device, mesh=mesh, in_specs=in_specs, out_specs=out_specs, check_vma=False
    )
```

profile of v0, /device:TPU:1, one launch (start us, length us, event | category | flops | bytes accessed | tf_op | source)
XLA Modules:
  0.0 671.4 jit_solution(17267883612236582695)
XLA Ops:
  7.2 0.7 convert_element_type.3
  8.8 24.9 %psum.70 = f32[32,32]{0,1:T(8,128)S(1)} all-reduce(f32[32,32]{0,1:T(8,128)S(1)} %fusion.14), channel_id=1, replica_groups=mesh['cell'=16,'gene'=8] {'gene'}, use_global_device_ids=true, to_apply=%region_0.0 | all-reduce | flops 1024 | bytes 8192 | tf_op jit(solution)/shard_map/psum | solution.py:58
  33.7 2.9 cholesky.59
  38.0 2.4 custom-call.7
  40.4 0.7 convolution_bitcast_fusion.2
  41.1 11.6 %mul.17 = f32[6,256,16,256]{3,2,1,0:T(8,128)} broadcast(f32[6,16]{1,0:T(8,128)S(1)} %convert_element_type.3), dimensions={0,2} | broadcast | bytes 25166208 | tf_op jit(solution)/shard_map/mul | solution.py:34
  52.6 27.6 %copy.16 = f32[192,8,16,256]{3,1,2,0:T(8,128)S(1)} copy(f32[192,8,16,256]{3,2,1,0:T(8,128)} %bitcast.98) | data formatting | bytes 50331648
  80.3 18.8 %fusion.13 = (f32[4096]{0:T(1024)S(1)}, f32[1536,4096]{1,0:T(8,128)}) fusion(f32[1536,4096]{1,0:T(8,128)} %param.6, f32[1536,4096]{1,0:T(8,128)S(1)} %bitcast.97), kind=kLoop, calls=%fused_computation.49 | loop fusion | flops 12578816 | bytes 75513856 | tf_op jit(solution)/shard_map/reduce_sum | solution.py:56
  99.0 60.7 %psum.71 = f32[4096]{0:T(1024)S(1)} all-reduce(f32[4096]{0:T(1024)S(1)} %get-tuple-element.8), channel_id=1, replica_groups=mesh['cell'=16,'gene'=8] {'cell'}, use_global_device_ids=true, to_apply=%region_4.7 | all-reduce | flops 4096 | bytes 32768 | tf_op jit(solution)/shard_map/psum | solution.py:56
  160.3 23.5 %convolution_subtract_fusion.4 = f32[1536,32]{1,0:T(8,128)} fusion(f32[1536,4096]{1,0:T(8,128)} %get-tuple-element.9, f32[4096,32]{0,1:T(8,128)S(1)} %convolution_bitcast_fusion.2, f32[32]{0:T(128)S(1)} %convolution_bitcast_fusion.7), kind=kOutput, calls=%fused_computation.10 | convolution fusion | flops 2415968256 | bytes 25886848 | tf_op jit(solution)/shard_map/dot_general | solution.py:22
  183.9 70.1 %all-reduce.5.cloned.1.call-done = f32[1536,32]{1,0:T(8,128)} async-done(((f32[1536,32]{1,0:T(8,128)}), f32[1536,32]{1,0:T(8,128)}) %all-reduce.5.cloned.1.call-update) | async-done | bytes 196624 | tf_op jit(solution)/shard_map/psum | solution.py:65
  254.0 18.8 %convolution_multiply_fusion.1 = f32[4096,32]{0,1:T(8,128)} fusion(f32[1536,4096]{1,0:T(8,128)} %get-tuple-element.9, f32[1536,32]{1,0:T(8,128)} %all-reduce.5.cloned.1.call-done), kind=kOutput, calls=%fused_computation.8 | convolution fusion | flops 2416050176 | bytes 25886720 | tf_op jit(solution)/shard_map/dot_general | solution.py:16
  272.9 84.9 %all-reduce.7.cloned.1.call-done = f32[4096,32]{0,1:T(8,128)} async-done(((f32[4096,32]{0,1:T(8,128)}), f32[4096,32]{0,1:T(8,128)}) %all-reduce.7.cloned.1.call-update) | async-done | bytes 524304 | tf_op jit(solution)/shard_map/psum | solution.py:66
  357.7 1.6 convolution_bitcast_fusion.5
  359.3 22.9 %psum.74 = f32[1,32,32]{2,1,0:T(8,128)S(1)} all-reduce(f32[1,32,32]{2,1,0:T(8,128)S(1)} %convolution_bitcast_fusion.5), channel_id=1, replica_groups=mesh['cell'=16,'gene'=8] {'gene'}, use_global_device_ids=true, to_apply=%region_7.10 | all-reduce | flops 1024 | bytes 8192 | tf_op jit(solution)/shard_map/psum | solution.py:41
  382.3 1.7 convolution_subtract_fusion.2
  384.5 23.8 %psum.75 = f32[32,32]{0,1:T(8,128)S(1)} all-reduce(f32[32,32]{0,1:T(8,128)S(1)} %fusion.15), channel_id=1, replica_groups=mesh['cell'=16,'gene'=8] {'gene'}, use_global_device_ids=true, to_apply=%region_8.11 | all-reduce | flops 1024 | bytes 8192 | tf_op jit(solution)/shard_map/psum | solution.py:45
  408.3 2.9 cholesky.70
  412.6 2.4 custom-call.8
  416.2 23.6 %convolution_subtract_fusion.3 = f32[1536,32]{1,0:T(8,128)} fusion(f32[1536,4096]{1,0:T(8,128)} %get-tuple-element.9, f32[4096,32]{0,1:T(8,128)S(1)} %convolution_bitcast_fusion.1, f32[32]{0:T(128)S(1)} %convolution_bitcast_fusion.6), kind=kOutput, calls=%fused_computation.9 | convolution fusion | flops 2415968256 | bytes 25886848 | tf_op jit(solution)/shard_map/dot_general | solution.py:22
  439.9 59.1 %all-reduce.9.cloned.1.call-done = f32[1536,32]{1,0:T(8,128)} async-done(((f32[1536,32]{1,0:T(8,128)}), f32[1536,32]{1,0:T(8,128)}) %all-reduce.9.cloned.1.call-update) | async-done | bytes 196624 | tf_op jit(solution)/shard_map/psum | solution.py:65
  499.0 18.8 %convolution_multiply_fusion = f32[4096,32]{0,1:T(8,128)} fusion(f32[1536,4096]{1,0:T(8,128)} %get-tuple-element.9, f32[1536,32]{1,0:T(8,128)} %all-reduce.9.cloned.1.call-done), kind=kOutput, calls=%fused_computation.7 | convolution fusion | flops 2416050176 | bytes 25886720 | tf_op jit(solution)/shard_map/dot_general | solution.py:16
  517.8 84.9 %all-reduce.11.cloned.1.call-done = f32[4096,32]{0,1:T(8,128)} async-done(((f32[4096,32]{0,1:T(8,128)}), f32[4096,32]{0,1:T(8,128)}) %all-reduce.11.cloned.1.call-update) | async-done | bytes 524304 | tf_op jit(solution)/shard_map/psum | solution.py:66
  602.7 1.6 convolution_bitcast_fusion.3
  604.3 1.6 convolution_bitcast_fusion.4
  606.0 23.0 %psum.78 = f32[2,32,32]{2,1,0:T(8,128)S(1)} all-reduce(f32[2,32,32]{2,1,0:T(8,128)S(1)} %pad_maximum_fusion), channel_id=1, replica_groups=mesh['cell'=16,'gene'=8] {'gene'}, use_global_device_ids=true, to_apply=%region_11.14 | all-reduce | flops 2048 | bytes 16384 | tf_op jit(solution)/shard_map/psum | solution.py:41
  628.9 1.7 convolution_subtract_fusion.1
  632.4 23.6 %psum.79 = f32[32,32]{0,1:T(8,128)S(1)} all-reduce(f32[32,32]{0,1:T(8,128)S(1)} %fusion.16), channel_id=1, replica_groups=mesh['cell'=16,'gene'=8] {'gene'}, use_global_device_ids=true, to_apply=%region_12.15 | all-reduce | flops 1024 | bytes 8192 | tf_op jit(solution)/shard_map/psum | solution.py:45
  656.1 2.9 cholesky.81
  660.3 2.4 custom-call.9
  662.7 1.4 fusion
  664.2 0.7 copy.12
  (39 shorter events, 9.3 us)
Async XLA Ops:
  7.2 1.1 copy-start
  7.2 246.8 %all-reduce.5.cloned.1.call-start = ((), (), s32[]{:S(2)}) async-start(), calls=%async_computation | async-start | bytes 1572864 | tf_op jit(solution)/shard_map/psum | solution.py:65
  183.8 173.9 %all-reduce.7.cloned.1.call-start = ((), (), s32[]{:S(2)}) async-start(), calls=%async_computation.1 | async-start | bytes 1048576 | tf_op jit(solution)/shard_map/psum | solution.py:66
  272.8 226.1 %all-reduce.9.cloned.1.call-start = ((), (), s32[]{:S(2)}) async-start(), calls=%async_computation.2 | async-start | bytes 1572864 | tf_op jit(solution)/shard_map/psum | solution.py:65
  416.2 248.7 %copy-start.1 = (f32[4096,32]{0,1:T(8,128)S(1)}, f32[4096,32]{0,1:T(8,128)}, u32[]{:S(2)}) copy-start(f32[4096,32]{0,1:T(8,128)} %param.8) | copy-start | bytes 1572868
  439.8 162.9 %all-reduce.11.cloned.1.call-start = ((), (), s32[]{:S(2)}) async-start(), calls=%async_computation.3 | async-start | bytes 1048576 | tf_op jit(solution)/shard_map/psum | solution.py:66
Sparse Core Ops, SparseCore 0:
  183.9 69.9 all-reduce.4
  272.9 84.7 all-reduce.6
  440.0 58.9 all-reduce.8
  517.9 84.7 all-reduce.10
where the time goes:
time: 674 us; the launch traced here: 671 us
  waiting for transfers between devices  299 us (44%)
  blocking collectives  179 us (27%)
  matrix products  98.9 us (15%)
  local copies, waits for them, and re-layouts  40.4 us (6%)
  other arithmetic  40.2 us (6%)
  between operations  13.9 us (2%)
    psum x2, waiting for transfers between devices, per_device(): image = lax.psum(transposed_dot(masked, cell_side) / cells, 'cell')  170 us
    psum x2, waiting for transfers between devices, per_device(): cell_side = lax.psum(partial_side, 'gene')  129 us
    psum x1, blocking collectives, per_device(): means = lax.psum(jnp.sum(masked, axis=0), 'cell') / cells  60.7 us
    dot_general x7, matrix products, product(): jnp.dot(left, right, precision=highest, preferred_element_type=jnp.float32)  52.1 us
    psum x2, blocking collectives, orthogonalize(): gram = lax.psum(transposed_dot(resid, resid), 'gene')  47.3 us
    psum x2, blocking collectives, orthogonalize(): summed = lax.psum(jnp.stack(projections), 'gene')  45.9 us
    dot_general x8, matrix products, transposed_dot(): lax.dot_general(left, right, (((0,), (0,)), ((), ())), precision=highest,...  44.1 us
    unnamed x6, local copies, waits for them, and re-layouts  28.6 us
  transfers between devices with their start and end apart: 4, of which 4 were waited for; matrix products, arithmetic and copies ran while one was open for 0% of the time, Pallas kernels for 0%

commit v1 on v0

v1 whole, which is shorter than its diff:
```python
import functools
import math

import jax
import jax.numpy as jnp
from jax import lax
from jax.experimental import pallas as pl
from jax.experimental.pallas import tpu as pltpu
from jax.sharding import PartitionSpec as P

TILE = 256
BLOCK = 32
MESH = pl.DeviceIdType.MESH
F32 = jnp.float32
BF16 = jnp.bfloat16
HIGHEST = lax.Precision.HIGHEST


def dot(left, right, dims, precision=None):
    return lax.dot_general(left, right, (dims, ((), ())), precision=precision, preferred_element_type=F32)


NN = ((1,), (0,))
NT = ((1,), (1,))


def split3(value):
    first = value.astype(BF16)
    rest = value - first.astype(F32)
    second = rest.astype(BF16)
    third = (rest - second.astype(F32)).astype(BF16)
    return jnp.concatenate([first, second, third], axis=0)


def fold3(value):
    return value[0:BLOCK] + value[BLOCK : 2 * BLOCK] + value[2 * BLOCK : 3 * BLOCK]


def factor(gram):
    row_of = lax.broadcasted_iota(jnp.int32, (BLOCK, 128), 0)
    lane_of = lax.broadcasted_iota(jnp.int32, (BLOCK, 128), 1)
    both = jnp.concatenate([gram, jnp.zeros((BLOCK, 128 - BLOCK), F32)], axis=1)
    both = both + (lane_of == row_of + BLOCK).astype(F32)
    for k in range(BLOCK - 1):
        row = both[k : k + 1, :]
        scaled = row / row[:, k : k + 1]
        column = jnp.where(row_of[:, 0:1] > k, both[:, k : k + 1], 0.0)
        both = both - column * scaled
    diagonal = jnp.sum(jnp.where(lane_of == row_of, both, 0.0), axis=1, keepdims=True)
    both = both / jnp.sqrt(diagonal)
    upper = jnp.where(lane_of >= row_of, both, 0.0)
    return upper[:, 0:BLOCK], both[:, BLOCK : 2 * BLOCK]


def kernel(
    sizes,
    x_ref,
    mask_ref,
    start_ref,
    alphas_ref,
    betas_ref,
    next_ref,
    high,
    low,
    stage,
    start3,
    gram_buf,
    z_send,
    z_recv,
    z_full,
    z_send2,
    z_recv2,
    z_full2,
    y_all,
    y3,
    stat_buf,
    i_send,
    i_recv,
    i_send2,
    i_recv2,
    resid,
    acc,
    load_sem,
    gram_send_sem,
    gram_sem,
    z_send_sem,
    z_sem,
    zg_send_sem,
    zg_sem,
    z2_sems,
    stat_send_sem,
    stat_sem,
    rs_send_sem,
    rs_sem,
    ag_send_sem,
    ag_sem,
):
    n_cell, n_gene, rows, width = sizes
    cells = rows * n_cell
    chunks = rows // TILE
    tiles = width // TILE
    c = lax.axis_index("cell")
    g = lax.axis_index("gene")
    z, core = g // 2, g % 2

    def load(i, slot):
        return pltpu.make_async_copy(
            x_ref.at[pl.ds(pl.multiple_of(i * TILE, TILE), TILE), :], stage.at[slot], load_sem.at[slot]
        )

    for i in range(3):
        load(i, i).start()

    barrier = pltpu.get_barrier_semaphore()

    @pl.loop(1, n_cell)
    def _(k):
        pl.semaphore_signal(barrier, inc=1, device_id=(lax.rem(c + k, n_cell), g), device_id_type=MESH)

    @pl.loop(1, n_gene)
    def _(k):
        pl.semaphore_signal(barrier, inc=1, device_id=(c, lax.rem(g + k, n_gene)), device_id_type=MESH)

    def pad_lanes(value):
        return jnp.concatenate([value, jnp.zeros((value.shape[0], 128 - value.shape[1]), F32)], axis=1)

    def send_gram(step, value):
        gram_buf[step, g] = pad_lanes(value)

        @pl.loop(1, n_gene)
        def _(k):
            pltpu.make_async_remote_copy(
                src_ref=gram_buf.at[step, g],
                dst_ref=gram_buf.at[step, g],
                send_sem=gram_send_sem.at[step],
                recv_sem=gram_sem.at[step],
                device_id=(c, lax.rem(g + k, n_gene)),
                device_id_type=MESH,
            ).start()

    def take_gram(step):
        part = gram_buf.at[step, pl.ds(0, n_gene - 1)]
        pltpu.make_async_copy(part, part, gram_sem.at[step]).wait()
        total = gram_buf[step, 0]
        for k in range(1, n_gene):
            total = total + gram_buf[step, k]
        return total[:, 0:BLOCK]

    start3[...] = split3(start_ref[...])
    gram0 = dot(start_ref[...], start_ref[...], NT, HIGHEST)
    pl.semaphore_wait(barrier, n_cell + n_gene - 2)
    send_gram(0, gram0)

    def spread(i):
        @pl.loop(1, n_gene)
        def _(k):
            peer = lax.rem(g + k, n_gene)
            pltpu.make_async_remote_copy(
                src_ref=z_send.at[
                    i, pl.ds(pl.multiple_of(peer // 2 * 8, 8), 8), pl.ds(pl.multiple_of(peer % 2 * 128, 128), 128)
                ],
                dst_ref=z_recv.at[i, k],
                send_sem=z_send_sem.at[i],
                recv_sem=z_sem.at[i],
                device_id=(c, peer),
                device_id_type=MESH,
            ).start()

    def gather(i):
        part = z_recv.at[i, pl.ds(1, n_gene - 1)]
        pltpu.make_async_copy(part, part, z_sem.at[i]).wait()
        own_rows = pl.ds(pl.multiple_of(z * 8, 8), 8)
        total = z_send[i, own_rows, pl.ds(pl.multiple_of(core * 128, 128), 128)]
        for k in range(1, n_gene):
            total = total + z_recv[i, k]
        place = z_full.at[own_rows, pl.ds(pl.multiple_of(i * TILE + core * 128, 128), 128)]
        place[...] = total

        @pl.loop(1, n_gene)
        def _(k):
            pltpu.make_async_remote_copy(
                src_ref=place,
                dst_ref=place,
                send_sem=zg_send_sem.at[0],
                recv_sem=zg_sem.at[0],
                device_id=(c, lax.rem(g + k, n_gene)),
                device_id_type=MESH,
            ).start()

    @pl.loop(0, chunks)
    def _(i):
        slot = lax.rem(i, 3)
        load(i, slot).wait()
        here = pl.ds(pl.multiple_of(i * TILE, TILE), TILE)

        def tile(j, total):
            lanes = pl.ds(pl.multiple_of(j * TILE, TILE), TILE)
            values = stage[slot, :, lanes] * mask_ref[i, j].astype(F32)
            top = values.astype(BF16)
            rest = (values - top.astype(F32)).astype(BF16)
            high[here, lanes] = top
            low[here, lanes] = rest
            return total + dot(start3[:, lanes], top, NT) + dot(start3[:, lanes], rest, NT)

        total = lax.fori_loop(0, tiles, tile, jnp.zeros((3 * BLOCK, TILE), F32))

        @pl.when(i + 3 < chunks)
        def _():
            load(i + 3, slot).start()

        z_send[i] = fold3(total)
        spread(i)

        @pl.when(i > 0)
        def _():
            gather(i - 1)

    upper, inverse0 = factor(take_gram(0))
    gather(chunks - 1)
    pltpu.make_async_copy(
        z_recv.at[:, pl.ds(1, n_gene - 1)], z_recv.at[:, pl.ds(1, n_gene - 1)], zg_sem.at[0]
    ).wait()

    ones = jnp.ones((16, rows), BF16)
    y3[pl.ds(3 * BLOCK, 16), :] = ones
    y_all[pl.ds(2 * BLOCK, 8), :] = jnp.ones((8, rows), F32)
    y_all[pl.ds(BLOCK, BLOCK), :] = jnp.zeros((BLOCK, rows), F32)
    own = pl.ds(pl.multiple_of(c * TILE, TILE), TILE)
    current = dot(inverse0, start_ref[:, own], NN, HIGHEST)
    older = None
    inverse = inverse0
    column_sums = None

    for step in range(2):
        if step == 0:
            side = dot(inverse, z_full[...], NN, HIGHEST)
        else:
            y_all[pl.ds(BLOCK, BLOCK), :] = y_all[pl.ds(0, BLOCK), :]
            side = dot(inverse, z_full2[...], NN, HIGHEST)
        y_all[pl.ds(0, BLOCK), :] = side
        y3[pl.ds(0, 3 * BLOCK), :] = split3(side)
        stat = dot(jnp.concatenate([side, jnp.ones((8, rows), F32)], axis=0), y_all[...], NT, HIGHEST)
        stat_buf[step, c] = pad_lanes(stat)

        @pl.loop(1, n_cell)
        def _(k):
            pltpu.make_async_remote_copy(
                src_ref=stat_buf.at[step, c],
                dst_ref=stat_buf.at[step, c],
                send_sem=stat_send_sem.at[step],
                recv_sem=stat_sem.at[step],
                device_id=(lax.rem(c + k, n_cell), g),
                device_id_type=MESH,
            ).start()

        sent = i_send if step == 0 else i_send2
        got = i_recv if step == 0 else i_recv2
        left_rows = 3 * BLOCK + 16 if step == 0 else 3 * BLOCK

        def image(k):
            owner = lax.rem(c + k, n_cell)
            lanes = pl.ds(pl.multiple_of(owner * TILE, TILE), TILE)
            left = y3[pl.ds(0, left_rows), :]
            product = dot(left, high[:, lanes], NN) + dot(left, low[:, lanes], NN)
            sent[owner, pl.ds(0, BLOCK), :] = fold3(product)
            if step == 0:
                sent[owner, pl.ds(BLOCK, 8), :] = product[3 * BLOCK : 3 * BLOCK + 8]

        def send_image(k):
            owner = lax.rem(c + k, n_cell)
            pltpu.make_async_remote_copy(
                src_ref=sent.at[owner],
                dst_ref=got.at[k],
                send_sem=rs_send_sem.at[step],
                recv_sem=rs_sem.at[step],
                device_id=(owner, g),
                device_id_type=MESH,
            ).start()

        @pl.loop(0, n_cell // 2)
        def _(t):
            image(2 * t + 1)
            image(2 * t + 2)
            send_image(2 * t + 1)

            @pl.when(t < n_cell // 2 - 1)
            def _():
                send_image(2 * t + 2)

        part = stat_buf.at[step, pl.ds(0, n_cell - 1)]
        pltpu.make_async_copy(part, part, stat_sem.at[step]).wait()
        stat = stat_buf[step, 0]
        for k in range(1, n_cell):
            stat = stat + stat_buf[step, k]
        stat = stat / cells
        mean_column = stat[0:BLOCK, 2 * BLOCK : 2 * BLOCK + 1]
        mean_row = stat[BLOCK : BLOCK + 1, :]
        centered = stat[0:BLOCK, :] - mean_column * mean_row
        alpha = centered[:, 0:BLOCK]
        alphas_ref[step] = alpha

        part = got.at[pl.ds(1, n_cell - 1)]
        pltpu.make_async_copy(part, part, rs_sem.at[step]).wait()
        piece = sent[c]
        for k in range(1, n_cell):
            piece = piece + got[k]
        if step == 0:
            column_sums = piece[BLOCK : BLOCK + 1]
        piece = (piece[0:BLOCK] - mean_column * column_sums) / cells
        piece = piece - dot(alpha, current, NN, HIGHEST)
        if step > 0:
            piece = piece - dot(centered[:, BLOCK : 2 * BLOCK], older, NN, HIGHEST)
        resid[step, :, own] = piece

        @pl.loop(1, n_cell)
        def _(k):
            pltpu.make_async_remote_copy(
                src_ref=resid.at[step, :, own],
                dst_ref=resid.at[step, :, own],
                send_sem=ag_send_sem.at[step],
                recv_sem=ag_sem.at[step, k],
                device_id=(lax.rem(c + k, n_cell), g),
                device_id_type=MESH,
            ).start()

        def wait_piece(k):
            lanes = pl.ds(pl.multiple_of(lax.rem(c - k + n_cell, n_cell) * TILE, TILE), TILE)
            pltpu.make_async_copy(resid.at[step, :, lanes], resid.at[step, :, lanes], ag_sem.at[step, k]).wait()
            return lanes

        if step == 0:

            def multiply(lanes):
                left = split3(resid[step, :, lanes])
                return dot(left, high[:, lanes], NT) + dot(left, low[:, lanes], NT)

            acc[...] = multiply(own)

            @pl.loop(1, n_cell)
            def _(k):
                acc[...] += multiply(wait_piece(k))

            send_gram(1, dot(resid[step], resid[step], NT, HIGHEST))
            z_send2[...] = fold3(acc)
            half = rows // 2

            @pl.loop(1, n_gene)
            def _(k):
                peer = lax.rem(g + k, n_gene)
                pltpu.make_async_remote_copy(
                    src_ref=z_send2.at[
                        pl.ds(pl.multiple_of(peer // 2 * 8, 8), 8), pl.ds(pl.multiple_of(peer % 2 * half, half), half)
                    ],
                    dst_ref=z_recv2.at[k],
                    send_sem=z2_sems.at[0],
                    recv_sem=z2_sems.at[1],
                    device_id=(c, peer),
                    device_id_type=MESH,
                ).start()

            parts = z_recv2.at[pl.ds(1, n_gene - 1)]
            pltpu.make_async_copy(parts, parts, z2_sems.at[1]).wait()
            place = z_full2.at[
                pl.ds(pl.multiple_of(z * 8, 8), 8), pl.ds(pl.multiple_of(core * half, half), half)
            ]
            total = z_send2[pl.ds(pl.multiple_of(z * 8, 8), 8), pl.ds(pl.multiple_of(core * half, half), half)]
            for k in range(1, n_gene):
                total = total + z_recv2[k]
            place[...] = total

            @pl.loop(1, n_gene)
            def _(k):
                pltpu.make_async_remote_copy(
                    src_ref=place,
                    dst_ref=place,
                    send_sem=z2_sems.at[2],
                    recv_sem=z2_sems.at[3],
                    device_id=(c, lax.rem(g + k, n_gene)),
                    device_id_type=MESH,
                ).start()

            upper, inverse = factor(take_gram(1))
            betas_ref[0] = upper
            older = current
            current = dot(inverse, piece, NN, HIGHEST)
            pltpu.make_async_copy(parts, parts, z2_sems.at[3]).wait()
            for sem in (0, 2):
                pltpu.make_async_copy(parts, parts, z2_sems.at[sem]).wait()
        else:

            @pl.loop(1, n_cell)
            def _(k):
                wait_piece(k)

            send_gram(2, dot(resid[step], resid[step], NT, HIGHEST))
            upper, inverse = factor(take_gram(2))
            betas_ref[1] = upper
            next_ref[...] = dot(inverse * math.sqrt(width * n_gene), resid[step], NN, HIGHEST)

    for step in range(3):
        part = gram_buf.at[step, pl.ds(0, n_gene - 1)]
        pltpu.make_async_copy(part, part, gram_send_sem.at[step]).wait()
    for i in range(chunks):
        part = z_recv.at[i, pl.ds(1, n_gene - 1)]
        pltpu.make_async_copy(part, part, z_send_sem.at[i]).wait()
    part = z_recv.at[:, pl.ds(1, n_gene - 1)]
    pltpu.make_async_copy(part, part, zg_send_sem.at[0]).wait()
    for step in range(2):
        part = stat_buf.at[step, pl.ds(0, n_cell - 1)]
        pltpu.make_async_copy(part, part, stat_send_sem.at[step]).wait()
        part = (i_recv if step == 0 else i_recv2).at[pl.ds(1, n_cell - 1)]
        pltpu.make_async_copy(part, part, rs_send_sem.at[step]).wait()
        part = resid.at[step, :, pl.ds(0, (n_cell - 1) * TILE)]
        pltpu.make_async_copy(part, part, ag_send_sem.at[step]).wait()


def per_device(sizes, expression, tile_mask, start):
    n_cell, n_gene, rows, width = sizes
    chunks = rows // TILE
    vmem = pl.BlockSpec(memory_space=pltpu.VMEM)
    dma = pltpu.SemaphoreType.DMA
    alphas, betas, fresh = pl.pallas_call(
        functools.partial(kernel, sizes),
        out_shape=(
            jax.ShapeDtypeStruct((2, BLOCK, BLOCK), F32),
            jax.ShapeDtypeStruct((2, BLOCK, BLOCK), F32),
            jax.ShapeDtypeStruct((BLOCK, width), F32),
        ),
        in_specs=[pl.BlockSpec(memory_space=pl.ANY), pl.BlockSpec(memory_space=pltpu.SMEM), vmem],
        out_specs=(vmem, vmem, vmem),
        scratch_shapes=[
            pltpu.VMEM((rows, width), BF16),
            pltpu.VMEM((rows, width), BF16),
            pltpu.VMEM((3, TILE, width), F32),
            pltpu.VMEM((3 * BLOCK, width), BF16),
            pltpu.VMEM((3, n_gene, BLOCK, 128), F32),
            pltpu.VMEM((chunks, BLOCK, TILE), F32),
            pltpu.VMEM((chunks, n_gene, 8, 128), F32),
            pltpu.VMEM((BLOCK, rows), F32),
            pltpu.VMEM((BLOCK, rows), F32),
            pltpu.VMEM((n_gene, 8, rows // 2), F32),
            pltpu.VMEM((BLOCK, rows), F32),
            pltpu.VMEM((2 * BLOCK + 8, rows), F32),
            pltpu.VMEM((3 * BLOCK + 16, rows), BF16),
            pltpu.VMEM((2, n_cell, BLOCK + 8, 128), F32),
            pltpu.VMEM((n_cell, BLOCK + 8, TILE), F32),
            pltpu.VMEM((n_cell, BLOCK + 8, TILE), F32),
            pltpu.VMEM((n_cell, BLOCK, TILE), F32),
            pltpu.VMEM((n_cell, BLOCK, TILE), F32),
            pltpu.VMEM((2, BLOCK, width), F32),
            pltpu.VMEM((3 * BLOCK, rows), F32),
            dma((3,)),
            dma((3,)),
            dma((3,)),
            dma((chunks,)),
            dma((chunks,)),
            dma((1,)),
            dma((1,)),
            dma((4,)),
            dma((2,)),
            dma((2,)),
            dma((2,)),
            dma((2,)),
            dma((2,)),
            dma((2, n_cell)),
        ],
        compiler_params=pltpu.CompilerParams(
            collective_id=0, has_side_effects=True, vmem_limit_bytes=60 * 2**20
        ),
        name="lanczos",
    )(expression, tile_mask, start.T)
    return alphas, betas, fresh.T


def solution(mesh):
    n_cell, n_gene = mesh.shape["cell"], mesh.shape["gene"]

    def run(expression, tile_mask, start):
        sizes = (n_cell, n_gene, expression.shape[0] // n_cell, expression.shape[1] // n_gene)
        return jax.shard_map(
            functools.partial(per_device, sizes),
            mesh=mesh,
            in_specs=(P("cell", "gene"), P("cell", "gene"), P("gene", None)),
            out_specs=(P(), P(), P("gene", None)),
            check_vma=False,
        )(expression, tile_mask, start)

    return run
```

time: 674 us -> 119 us (0.18)
  waiting for transfers between devices: 299 us -> 0 us
  blocking collectives: 179 us -> 0 us
  Pallas kernels: 0 us -> 113 us
  matrix products: 98.9 us -> 0 us
  other arithmetic: 40.2 us -> 0 us
  local copies, waits for them, and re-layouts: 40.4 us -> 4.62 us
  between operations: 13.9 us -> 0.64 us
    psum x4 -> x0, waiting for transfers between devices: 299 us -> none  [the longest x2 170 us: per_device(): image = lax.psum(transposed_dot(masked, cell_side) / cells, 'cell')]
    psum x6 -> x0, blocking collectives: 179 us -> none  [the longest x1 60.7 us: per_device(): means = lax.psum(jnp.sum(masked, axis=0), 'cell') / cells]
    pallas_call x0 -> x1, Pallas kernels: none -> 113 us  [per_device(): pl.pallas_call(functools.partial(kernel, sizes), out_shape=(jax.ShapeDtyp...]
    dot_general x15 -> x0, matrix products: 96.2 us -> none  [the longest x7 52.1 us: product(): jnp.dot(left, right, precision=highest, preferred_element_type=jnp.float32)]
    unnamed x6 -> x3, local copies, waits for them, and re-layouts: 28.6 us -> 4.62 us
    another operation x18 -> x0, other arithmetic: 20.7 us -> none  [the longest x9 10.8 us: finish(): lower = jnp.linalg.cholesky(gram)]
    reduce_sum x1 -> x0, other arithmetic: 18.8 us -> none  [per_device(): means = lax.psum(jnp.sum(masked, axis=0), 'cell') / cells]
    mul x1 -> x0, local copies, waits for them, and re-layouts: 11.6 us -> none  [expand_mask(): tiles * tile_mask.astype(jnp.float32)[:, None, :, None]]
  transfers between devices with their start and end apart: 4 -> 0, of which waited for: 4 -> 0; matrix products, arithmetic and copies ran while one was open for 0% -> 0% of each run, Pallas kernels for 0% -> 0%
where the time goes in v1:
time: 119 us
  Pallas kernels  113 us (95%)
  local copies, waits for them, and re-layouts  4.62 us (4%)
    pallas_call x1, Pallas kernels, per_device(): pl.pallas_call(functools.partial(kernel, sizes), out_shape=(jax.ShapeDtyp...  113 us
    unnamed x3, local copies, waits for them, and re-layouts  4.62 us

profile of v1, /device:TPU:1, one launch (start us, length us, event | category | flops | bytes accessed | tf_op | source)
XLA Modules:
  0.0 118.7 jit_solution(6556646444561513867)
XLA Ops:
  0.6 113.4 %lanczos.1 = (f32[2,32,32]{2,1,0:T(8,128)}, f32[2,32,32]{2,1,0:T(8,128)}, f32[32,4096]{1,0:T(8,128)}) custom-call(f32[1536,4096]{1,0:T(8,128)} %x_ref.1, s32[6,16]{1,0:T(8,128)} %mask_ref.1, f32[32,4096]{1,0:T(8,128)} %bitcast.2), custom_call_target="tpu_custom_call" | custom-call | tf_op jit(solution)/shard_map/lanczos/pallas_call | solution.py:422
  114.1 1.4 %copy.9 = f32[2,32,32]{2,1,0:T(8,128)} copy(f32[2,32,32]{2,1,0:T(8,128)} %get-tuple-element.12) | data formatting | bytes 16384
  115.5 1.4 %copy.10 = f32[2,32,32]{2,1,0:T(8,128)} copy(f32[2,32,32]{2,1,0:T(8,128)} %get-tuple-element.13) | data formatting | bytes 16384
  116.8 1.9 %copy.11 = f32[4096,32]{0,1:T(8,128)} copy(f32[4096,32]{0,1:T(8,128)} %bitcast.3) | data formatting | bytes 1048576

commit v2 on v1

v2 whole, which is shorter than its diff:
```python
import functools
import math

import jax
import jax.numpy as jnp
from jax import lax
from jax.experimental import pallas as pl
from jax.experimental.pallas import tpu as pltpu
from jax.sharding import PartitionSpec as P

TILE = 256
BLOCK = 32
MESH = pl.DeviceIdType.MESH
F32 = jnp.float32
BF16 = jnp.bfloat16
UNROLL = 4
EARLY = 3

NN = ((1,), (0,))
NT = ((1,), (1,))
SIDE = 4
ORDER = sorted(
    ((dy, dx) for dy in range(SIDE) for dx in range(SIDE)),
    key=lambda at: (min(at[0], SIDE - at[0]) + min(at[1], SIDE - at[1]), at),
)


def dot(left, right, dims):
    return lax.dot_general(left, right, (dims, ((), ())), preferred_element_type=F32)


def pieces(value):
    first = value.astype(BF16)
    rest = value - first.astype(F32)
    second = rest.astype(BF16)
    third = (rest - second.astype(F32)).astype(BF16)
    return first, second, third


def split3(value):
    return jnp.concatenate(pieces(value), axis=0)


def fold3(value):
    return value[0:BLOCK] + value[BLOCK : 2 * BLOCK] + value[2 * BLOCK : 3 * BLOCK]


def fold_lanes(value, at=0):
    a, b, d = (value[:, at + BLOCK * k : at + BLOCK * (k + 1)] for k in range(3))
    return a + b + d


def small_product(left, right):
    a1, a2, a3 = pieces(left)
    b1, b2, b3 = pieces(right)
    lhs = jnp.concatenate([a1, a2, a3, a1, a2, a1], axis=1)
    rhs = jnp.concatenate([b1, b1, b1, b2, b2, b3], axis=0)
    return dot(lhs, rhs, NN)


def gram_of(split):
    return fold_lanes(fold3(dot(split, split, NT)))


def pack(matrix):
    return jnp.concatenate([matrix[8 * k : 8 * (k + 1), :] for k in range(4)], axis=1)


def unpack(tile):
    return jnp.concatenate([tile[:, BLOCK * k : BLOCK * (k + 1)] for k in range(4)], axis=0)


def factor(gram):
    row_of = lax.broadcasted_iota(jnp.int32, (BLOCK, 128), 0)
    lane_of = lax.broadcasted_iota(jnp.int32, (BLOCK, 128), 1)
    both = jnp.concatenate([gram, jnp.zeros((BLOCK, 128 - BLOCK), F32)], axis=1)
    both = both + (lane_of == row_of + BLOCK).astype(F32)
    for k in range(BLOCK - 1):
        row = both[k : k + 1, :]
        scaled = row / row[:, k : k + 1]
        column = jnp.where(row_of[:, 0:1] > k, both[:, k : k + 1], 0.0)
        both = both - column * scaled
    diagonal = jnp.sum(jnp.where(lane_of == row_of, both, 0.0), axis=1, keepdims=True)
    both = both / jnp.sqrt(diagonal)
    upper = jnp.where(lane_of >= row_of, both, 0.0)
    return upper[:, 0:BLOCK], both[:, BLOCK : 2 * BLOCK]


def kernel(
    sizes,
    x_ref,
    mask_ref,
    start_ref,
    small_ref,
    resid_ref,
    high,
    low,
    stage,
    start3,
    gram_buf,
    last_buf,
    z_send,
    z_recv,
    z_full,
    z_send2,
    z_recv2,
    z_full2,
    y3,
    stat_buf,
    image_acc,
    i_send,
    i_recv,
    i_send2,
    i_recv2,
    resid,
    resid3,
    acc,
    load_sem,
    gram_sems,
    last_sems,
    z_send_sem,
    z_sem,
    zg_send_sem,
    zg_sem,
    z2_sems,
    stat_send_sem,
    stat_sem,
    rs_send_sem,
    rs_sem,
    ag_send_sem,
    ag_sem,
):
    n_cell, n_gene, rows, width = sizes
    cells = rows * n_cell
    chunks = rows // TILE
    tiles = width // TILE
    c = lax.axis_index("cell")
    g = lax.axis_index("gene")
    z, core = g // 2, g % 2
    y_at, x_at = c // SIDE, c % SIDE

    def cell_at(k, sign):
        if isinstance(k, int):
            dy, dx = ORDER[k]
        else:
            dy, dx = ORDER[0]
            for i in range(1, n_cell):
                dy = jnp.where(k == i, ORDER[i][0], dy)
                dx = jnp.where(k == i, ORDER[i][1], dx)
        return lax.rem(y_at + sign * dy + SIDE, SIDE) * SIDE + lax.rem(x_at + sign * dx + SIDE, SIDE)

    def block(index, size=TILE):
        return pl.ds(pl.multiple_of(index * size, size), size)

    def wait_bytes(ref, sem):
        pltpu.make_async_copy(ref, ref, sem).wait()

    def load(i, slot):
        return pltpu.make_async_copy(x_ref.at[block(i), :], stage.at[slot], load_sem.at[slot])

    for i in range(3):
        load(i, i).start()

    barrier = pltpu.get_barrier_semaphore()

    @pl.loop(1, n_cell)
    def _(k):
        pl.semaphore_signal(barrier, inc=1, device_id=(lax.rem(c + k, n_cell), g), device_id_type=MESH)

    @pl.loop(1, n_gene)
    def _(k):
        pl.semaphore_signal(barrier, inc=1, device_id=(c, lax.rem(g + k, n_gene)), device_id_type=MESH)

    def to_genes(src, dst, send_sem, recv_sem):
        @pl.loop(1, n_gene)
        def _(k):
            pltpu.make_async_remote_copy(
                src_ref=src,
                dst_ref=dst,
                send_sem=send_sem,
                recv_sem=recv_sem,
                device_id=(c, lax.rem(g + k, n_gene)),
                device_id_type=MESH,
            ).start()

    def to_cells(src, dst, send_sem, recv_sem_of):
        @pl.loop(1, n_cell)
        def _(t):
            k = n_cell - t
            pltpu.make_async_remote_copy(
                src_ref=src,
                dst_ref=dst,
                send_sem=send_sem,
                recv_sem=recv_sem_of(k),
                device_id=(cell_at(k, 1), g),
                device_id_type=MESH,
            ).start()

    def sum_slots(buf, count):
        total = buf[0]
        for k in range(1, count):
            total = total + buf[k]
        return total

    def send_gram(step, tile):
        gram_buf[step, g] = tile
        here = gram_buf.at[step, g]
        to_genes(here, here, gram_sems.at[step, 0], gram_sems.at[step, 1])

    def take_gram(step):
        wait_bytes(gram_buf.at[step, pl.ds(0, n_gene - 1)], gram_sems.at[step, 1])
        return unpack(sum_slots(gram_buf.at[step], n_gene))

    start3[...] = split3(start_ref[...])
    gram0 = pack(gram_of(start3[...]))
    y3[0, pl.ds(3 * BLOCK, 16), :] = jnp.ones((16, rows), BF16)
    y3[1, pl.ds(3 * BLOCK, 16), :] = jnp.ones((16, rows), BF16)
    pl.semaphore_wait(barrier, n_cell + n_gene - 2)
    send_gram(0, gram0)

    def spread(i):
        @pl.loop(1, n_gene)
        def _(k):
            peer = lax.rem(g + k, n_gene)
            pltpu.make_async_remote_copy(
                src_ref=z_send.at[i, block(peer // 2, 8), block(peer % 2, 128)],
                dst_ref=z_recv.at[i, k],
                send_sem=z_send_sem.at[i],
                recv_sem=z_sem.at[i],
                device_id=(c, peer),
                device_id_type=MESH,
            ).start()

    def gather(i):
        wait_bytes(z_recv.at[i, pl.ds(1, n_gene - 1)], z_sem.at[i])
        total = z_send[i, block(z, 8), block(core, 128)]
        for k in range(1, n_gene):
            total = total + z_recv[i, k]
        place = z_full.at[block(z, 8), pl.ds(pl.multiple_of(i * TILE + core * 128, 128), 128)]
        place[...] = total
        to_genes(place, place, zg_send_sem.at[i], zg_sem.at[i])

    @pl.loop(0, chunks)
    def _(i):
        slot = lax.rem(i, 3)
        load(i, slot).wait()
        here = block(i)

        def tile(j, total):
            lanes = block(j)
            values = stage[slot, :, lanes] * mask_ref[i, j].astype(F32)
            top = values.astype(BF16)
            rest = (values - top.astype(F32)).astype(BF16)
            high[here, lanes] = top
            low[here, lanes] = rest
            return total + dot(start3[:, lanes], top, NT) + dot(start3[:, lanes], rest, NT)

        total = lax.fori_loop(0, tiles, tile, jnp.zeros((3 * BLOCK, TILE), F32), unroll=UNROLL)

        @pl.when(i + 3 < chunks)
        def _():
            load(i + 3, slot).start()

        z_send[i] = fold3(total)
        spread(i)

        @pl.when(i > 0)
        def _():
            gather(i - 1)

    _, inverse0 = factor(take_gram(0))

    def side_of(step, inverse, full, first, count):
        lanes = pl.ds(first * TILE, count * TILE)
        y3[step, pl.ds(0, 3 * BLOCK), lanes] = split3(small_product(inverse, full[:, lanes]))

    def back(step, left_rows, first, count, lanes):
        there = pl.ds(first * TILE, count * TILE)
        left = y3[step, pl.ds(0, left_rows), there]
        return dot(left, high[there, lanes], NN) + dot(left, low[there, lanes], NN)

    with_ones = 3 * BLOCK + 16
    early, middle = EARLY, chunks - 1

    def wait_chunks(first, last):
        for i in range(first, last):
            wait_bytes(z_recv.at[i, pl.ds(1, n_gene - 1)], zg_sem.at[i])

    wait_chunks(0, early)
    side_of(0, inverse0, z_full, 0, early)

    @pl.loop(0, tiles // 2)
    def _(t):
        lanes = block(t, 2 * TILE)
        image_acc[:, lanes] = back(0, with_ones, 0, early, lanes)

    gather(chunks - 1)
    wait_chunks(early, middle)
    side_of(0, inverse0, z_full, early, middle - early)

    @pl.loop(0, tiles // 2)
    def _(t):
        lanes = block(t, 2 * TILE)
        image_acc[:, lanes] += back(0, with_ones, early, middle - early, lanes)

    own = block(c)
    current = small_product(inverse0, start_ref[:, own])
    older = None
    inverse = inverse0
    wait_chunks(middle, chunks)
    side_of(0, inverse0, z_full, middle, chunks - middle)
    eye = lax.broadcasted_iota(jnp.int32, (BLOCK, BLOCK), 0) == lax.broadcasted_iota(jnp.int32, (BLOCK, BLOCK), 1)
    column_sums = None
    older_mean = None

    for step in range(2):
        if step == 0:
            stat = dot(y3[0], y3[0], NT)
        else:
            stat = dot(y3[1], jnp.concatenate([y3[1], y3[0]], axis=0), NT)
        row = fold_lanes(stat[3 * BLOCK : 3 * BLOCK + 8])
        stat = fold3(stat)
        stat_buf[step, c, 0] = pack(fold_lanes(stat))
        stat_buf[step, c, 1] = jnp.concatenate([row, jnp.zeros((8, 128 - BLOCK), F32)], axis=1)
        count = 2
        if step == 1:
            stat_buf[step, c, 2] = pack(fold_lanes(stat, with_ones))
            count = 3
        here = stat_buf.at[step, c, pl.ds(0, count)]
        to_cells(here, here, stat_send_sem.at[step], lambda k: stat_sem.at[step])

        sent = i_send if step == 0 else i_send2
        got = i_recv if step == 0 else i_recv2

        def image(k):
            owner = cell_at(k, 1)
            lanes = block(owner)
            if step == 0:
                product = image_acc[:, lanes] + back(0, with_ones, middle, chunks - middle, lanes)
                sent[k, pl.ds(BLOCK, 8), :] = product[3 * BLOCK : 3 * BLOCK + 8]
            else:
                product = back(1, 3 * BLOCK, 0, chunks, lanes)
            sent[k, pl.ds(0, BLOCK), :] = fold3(product)
            return owner

        def send_image(k, owner):
            pltpu.make_async_remote_copy(
                src_ref=sent.at[k],
                dst_ref=got.at[k],
                send_sem=rs_send_sem.at[step],
                recv_sem=rs_sem.at[step],
                device_id=(owner, g),
                device_id_type=MESH,
            ).start()

        @pl.loop(0, n_cell // 2)
        def _(t):
            one, two = n_cell - 1 - 2 * t, n_cell - 2 - 2 * t
            owner_one = image(one)
            owner_two = image(two)
            send_image(one, owner_one)

            @pl.when(t < n_cell // 2 - 1)
            def _():
                send_image(two, owner_two)

        wait_bytes(stat_buf.at[step, pl.ds(0, n_cell - 1), pl.ds(0, count)], stat_sem.at[step])
        stats = [sum_slots(stat_buf.at[step, :, k], n_cell) / cells for k in range(count)]
        mean_row = stats[1][0:1, 0:BLOCK]
        mean_column = jnp.sum(jnp.where(eye, mean_row, 0.0), axis=1, keepdims=True)
        alpha = unpack(stats[0]) - mean_column * mean_row
        small_ref[1 + step] = alpha

        wait_bytes(got.at[pl.ds(1, n_cell - 1)], rs_sem.at[step])
        piece = sent[0]
        for k in range(1, n_cell):
            piece = piece + got[k]
        if step == 0:
            column_sums = piece[BLOCK : BLOCK + 1]
        piece = (piece[0:BLOCK] - mean_column * column_sums) / cells
        piece = piece - small_product(alpha, current)
        if step > 0:
            prior = unpack(stats[2]) - mean_column * older_mean
            piece = piece - small_product(prior, older)
        place = resid.at[step, :, own]
        place[...] = piece

        if step == 0:
            to_cells(place, place, ag_send_sem.at[step], lambda k: ag_sem.at[step, k])
            older_mean = mean_row

            def multiply(lanes):
                left = split3(resid[step, :, lanes])
                resid3[:, lanes] = left
                return dot(left, high[:, lanes], NT) + dot(left, low[:, lanes], NT)

            def arrived(k):
                lanes = block(cell_at(k, -1))
                wait_bytes(resid.at[step, :, lanes], ag_sem.at[step, k])
                return lanes

            acc[...] = multiply(own)

            @pl.loop(0, n_cell // 2 - 1)
            def _(t):
                one = arrived(2 * t + 1)
                two = arrived(2 * t + 2)
                acc[...] += multiply(one) + multiply(two)

            acc[...] += multiply(arrived(n_cell - 1))
            z_send2[...] = fold3(acc)
            half = rows // 2

            @pl.loop(1, n_gene)
            def _(k):
                peer = lax.rem(g + k, n_gene)
                pltpu.make_async_remote_copy(
                    src_ref=z_send2.at[block(peer // 2, 8), block(peer % 2, half)],
                    dst_ref=z_recv2.at[k],
                    send_sem=z2_sems.at[0],
                    recv_sem=z2_sems.at[1],
                    device_id=(c, peer),
                    device_id_type=MESH,
                ).start()

            send_gram(1, pack(gram_of(resid3[...])))
            parts = z_recv2.at[pl.ds(1, n_gene - 1)]
            wait_bytes(parts, z2_sems.at[1])
            total = z_send2[block(z, 8), block(core, half)]
            for k in range(1, n_gene):
                total = total + z_recv2[k]
            place = z_full2.at[block(z, 8), block(core, half)]
            place[...] = total
            to_genes(place, place, z2_sems.at[2], z2_sems.at[3])
            upper, inverse = factor(take_gram(1))
            small_ref[3] = upper
            older = current
            current = small_product(inverse, piece)
            wait_bytes(parts, z2_sems.at[3])
            wait_bytes(parts, z2_sems.at[0])
            wait_bytes(parts, z2_sems.at[2])
            side_of(1, inverse, z_full2, 0, chunks)
        else:
            last_buf[c] = pack(gram_of(split3(piece)))
            here = last_buf.at[c]
            to_cells(here, here, last_sems.at[0], lambda k: last_sems.at[1])
            to_cells(place, place, ag_send_sem.at[step], lambda k: ag_sem.at[step, 0])
            wait_bytes(last_buf.at[pl.ds(0, n_cell - 1)], last_sems.at[1])
            send_gram(2, sum_slots(last_buf, n_cell))
            wait_bytes(resid.at[step, :, pl.ds(0, (n_cell - 1) * TILE)], ag_sem.at[step, 0])
            resid_ref[...] = resid[step]
            upper, inverse = factor(take_gram(2))
            small_ref[0] = inverse
            small_ref[4] = upper

    for step in range(3):
        wait_bytes(gram_buf.at[step, pl.ds(0, n_gene - 1)], gram_sems.at[step, 0])
    wait_bytes(last_buf.at[pl.ds(0, n_cell - 1)], last_sems.at[0])
    for i in range(chunks):
        wait_bytes(z_recv.at[i, pl.ds(1, n_gene - 1)], z_send_sem.at[i])
        wait_bytes(z_recv.at[i, pl.ds(1, n_gene - 1)], zg_send_sem.at[i])
    for step in range(2):
        wait_bytes(stat_buf.at[step, pl.ds(0, n_cell - 1), pl.ds(0, 2 + step)], stat_send_sem.at[step])
        wait_bytes((i_recv if step == 0 else i_recv2).at[pl.ds(1, n_cell - 1)], rs_send_sem.at[step])
        wait_bytes(resid.at[step, :, pl.ds(0, (n_cell - 1) * TILE)], ag_send_sem.at[step])


def finish(scale, small_ref, resid_ref, alphas_ref, betas_ref, next_ref):
    next_ref[...] = small_product(small_ref[0] * scale, resid_ref[...])
    alphas_ref[...] = small_ref[1:3]
    betas_ref[...] = small_ref[3:5]


def per_device(sizes, expression, tile_mask, start):
    n_cell, n_gene, rows, width = sizes
    chunks = rows // TILE
    vmem = pl.BlockSpec(memory_space=pltpu.VMEM)
    dma = pltpu.SemaphoreType.DMA
    small, resid = pl.pallas_call(
        functools.partial(kernel, sizes),
        out_shape=(
            jax.ShapeDtypeStruct((5, BLOCK, BLOCK), F32),
            jax.ShapeDtypeStruct((BLOCK, width), F32),
        ),
        in_specs=[pl.BlockSpec(memory_space=pl.ANY), pl.BlockSpec(memory_space=pltpu.SMEM), vmem],
        out_specs=(vmem, vmem),
        scratch_shapes=[
            pltpu.VMEM((rows, width), BF16),
            pltpu.VMEM((rows, width), BF16),
            pltpu.VMEM((3, TILE, width), F32),
            pltpu.VMEM((3 * BLOCK, width), BF16),
            pltpu.VMEM((3, n_gene, 8, 128), F32),
            pltpu.VMEM((n_cell, 8, 128), F32),
            pltpu.VMEM((chunks, BLOCK, TILE), F32),
            pltpu.VMEM((chunks, n_gene, 8, 128), F32),
            pltpu.VMEM((BLOCK, rows), F32),
            pltpu.VMEM((BLOCK, rows), F32),
            pltpu.VMEM((n_gene, 8, rows // 2), F32),
            pltpu.VMEM((BLOCK, rows), F32),
            pltpu.VMEM((2, 3 * BLOCK + 16, rows), BF16),
            pltpu.VMEM((2, n_cell, 3, 8, 128), F32),
            pltpu.VMEM((3 * BLOCK + 16, width), F32),
            pltpu.VMEM((n_cell, BLOCK + 8, TILE), F32),
            pltpu.VMEM((n_cell, BLOCK + 8, TILE), F32),
            pltpu.VMEM((n_cell, BLOCK, TILE), F32),
            pltpu.VMEM((n_cell, BLOCK, TILE), F32),
            pltpu.VMEM((2, BLOCK, width), F32),
            pltpu.VMEM((3 * BLOCK, width), BF16),
            pltpu.VMEM((3 * BLOCK, rows), F32),
            dma((3,)),
            dma((3, 2)),
            dma((2,)),
            dma((chunks,)),
            dma((chunks,)),
            dma((chunks,)),
            dma((chunks,)),
            dma((4,)),
            dma((2,)),
            dma((2,)),
            dma((2,)),
            dma((2,)),
            dma((2,)),
            dma((2, n_cell)),
        ],
        compiler_params=pltpu.CompilerParams(
            collective_id=0, has_side_effects=True, vmem_limit_bytes=60 * 2**20
        ),
        name="lanczos",
    )(expression, tile_mask, start.T)
    alphas, betas, fresh = pl.pallas_call(
        functools.partial(finish, math.sqrt(width * n_gene)),
        out_shape=(
            jax.ShapeDtypeStruct((2, BLOCK, BLOCK), F32),
            jax.ShapeDtypeStruct((2, BLOCK, BLOCK), F32),
            jax.ShapeDtypeStruct((BLOCK, width), F32),
        ),
        in_specs=[vmem, vmem],
        out_specs=(vmem, vmem, vmem),
        name="finish",
    )(small, resid)
    return alphas, betas, fresh.T


def solution(mesh):
    n_cell, n_gene = mesh.shape["cell"], mesh.shape["gene"]

    def run(expression, tile_mask, start):
        sizes = (n_cell, n_gene, expression.shape[0] // n_cell, expression.shape[1] // n_gene)
        return jax.shard_map(
            functools.partial(per_device, sizes),
            mesh=mesh,
            in_specs=(P("cell", "gene"), P("cell", "gene"), P("gene", None)),
            out_specs=(P(), P(), P("gene", None)),
            check_vma=False,
        )(expression, tile_mask, start)

    return run
```

time: 119 us -> 104 us (0.87)
  Pallas kernels: 113 us -> 102 us
  local copies, waits for them, and re-layouts: 4.62 us -> 0 us
    pallas_call x1, Pallas kernels: 113 us -> 99.9 us  [per_device(): pl.pallas_call(functools.partial(kernel, sizes), out_shape=(jax.ShapeDtyp...]
    unnamed x3 -> x0, local copies, waits for them, and re-layouts: 4.62 us -> none
    pallas_call x0 -> x1, Pallas kernels: none -> 2.35 us  [per_device(): pl.pallas_call(functools.partial(finish, math.sqrt(width * n_gene)), out_...]
where the time goes in v2:
time: 104 us; the launch traced here: 103 us
  Pallas kernels  102 us (98%)
    pallas_call x1, Pallas kernels, per_device(): pl.pallas_call(functools.partial(kernel, sizes), out_shape=(jax.ShapeDtyp...  99.9 us
    pallas_call x1, Pallas kernels, per_device(): pl.pallas_call(functools.partial(finish, math.sqrt(width * n_gene)), out_...  2.35 us

profile of v2, /device:TPU:1, one launch (start us, length us, event | category | flops | bytes accessed | tf_op | source)
XLA Modules:
  0.0 102.8 jit_solution(4780874614724999398)
XLA Ops:
  0.6 99.9 %lanczos.1 = (f32[5,32,32]{2,1,0:T(8,128)}, f32[32,4096]{1,0:T(8,128)}) custom-call(f32[1536,4096]{1,0:T(8,128)} %x_ref.1, s32[6,16]{1,0:T(8,128)} %mask_ref.1, f32[32,4096]{1,0:T(8,128)} %bitcast.2), custom_call_target="tpu_custom_call" | custom-call | tf_op jit(solution)/shard_map/lanczos/pallas_call | solution.py:479
  100.5 2.3 %finish.1 = (f32[2,32,32]{2,1,0:T(8,128)}, f32[2,32,32]{2,1,0:T(8,128)}, f32[32,4096]{1,0:T(8,128)}) custom-call(f32[5,32,32]{2,1,0:T(8,128)} %get-tuple-element.8.small_ref, f32[32,4096]{1,0:T(8,128)} %get-tuple-element.9.resid_ref), custom_call_target="tpu_custom_call" | custom-call | tf_op jit(solution)/shard_map/finish/pallas_call | solution.py:530

commit v3 on v2

--- a/solution.py
+++ b/solution.py
@@ -13,8 +13,9 @@
 MESH = pl.DeviceIdType.MESH
 F32 = jnp.float32
 BF16 = jnp.bfloat16
-UNROLL = 4
-EARLY = 3
+FP8 = jnp.float8_e4m3fn
+LOW_SCALE = 4096.0
+GROUPS = ((0, 4), (4, 2))
 
 NN = ((1,), (0,))
 NT = ((1,), (1,))
@@ -35,6 +36,22 @@
     second = rest.astype(BF16)
     third = (rest - second.astype(F32)).astype(BF16)
     return first, second, third
+
+
+def pieces8(value, scale):
+    value = value * scale
+    first = value.astype(FP8)
+    second = ((value - first.astype(F32)) * 16.0).astype(FP8)
+    return jnp.concatenate([first, second], axis=0)
+
+
+def fold8(value):
+    return value[0:BLOCK] + value[BLOCK : 2 * BLOCK] * (1.0 / 16.0)
+
+
+def largest(values):
+    top = functools.reduce(jnp.maximum, [jnp.max(jnp.abs(v), axis=0, keepdims=True) for v in values])
+    return jnp.maximum(jnp.max(top, axis=1, keepdims=True), 1e-30)
 
 
 def split3(value):
@@ -97,15 +114,18 @@
     low,
     stage,
     start3,
+    start8,
     gram_buf,
     last_buf,
     z_send,
     z_recv,
+    z_recv_b,
     z_full,
     z_send2,
     z_recv2,
     z_full2,
     y3,
+    y8,
     stat_buf,
     image_acc,
     i_send,
@@ -114,7 +134,7 @@
     i_recv2,
     resid,
     resid3,
-    acc,
+    resid8,
     load_sem,
     gram_sems,
     last_sems,
@@ -212,103 +232,116 @@
         return unpack(sum_slots(gram_buf.at[step], n_gene))
 
     start3[...] = split3(start_ref[...])
+    start8[...] = pieces8(start_ref[...], 64.0)
     gram0 = pack(gram_of(start3[...]))
     y3[0, pl.ds(3 * BLOCK, 16), :] = jnp.ones((16, rows), BF16)
     y3[1, pl.ds(3 * BLOCK, 16), :] = jnp.ones((16, rows), BF16)
+    y8[pl.ds(2 * BLOCK, BLOCK), :] = jnp.ones((BLOCK, rows), FP8)
     pl.semaphore_wait(barrier, n_cell + n_gene - 2)
     send_gram(0, gram0)
 
-    def spread(i):
+    z_parts = (z_recv, z_recv_b)
+
+    def spread(n):
+        first, count = GROUPS[n]
+        half = count * 128
+
         @pl.loop(1, n_gene)
         def _(k):
             peer = lax.rem(g + k, n_gene)
             pltpu.make_async_remote_copy(
-                src_ref=z_send.at[i, block(peer // 2, 8), block(peer % 2, 128)],
-                dst_ref=z_recv.at[i, k],
-                send_sem=z_send_sem.at[i],
-                recv_sem=z_sem.at[i],
+                src_ref=z_send.at[
+                    block(peer // 2, 8), pl.ds(pl.multiple_of(first * TILE + peer % 2 * half, 128), half)
+                ],
+                dst_ref=z_parts[n].at[k],
+                send_sem=z_send_sem.at[n],
+                recv_sem=z_sem.at[n],
                 device_id=(c, peer),
                 device_id_type=MESH,
             ).start()
 
-    def gather(i):
-        wait_bytes(z_recv.at[i, pl.ds(1, n_gene - 1)], z_sem.at[i])
-        total = z_send[i, block(z, 8), block(core, 128)]
+    def gather(n):
+        first, count = GROUPS[n]
+        half = count * 128
+        wait_bytes(z_parts[n].at[pl.ds(1, n_gene - 1)], z_sem.at[n])
+        there = (block(z, 8), pl.ds(pl.multiple_of(first * TILE + core * half, 128), half))
+        total = z_send[there]
         for k in range(1, n_gene):
-            total = total + z_recv[i, k]
-        place = z_full.at[block(z, 8), pl.ds(pl.multiple_of(i * TILE + core * 128, 128), 128)]
+            total = total + z_parts[n][k]
+        place = z_full.at[there]
         place[...] = total
-        to_genes(place, place, zg_send_sem.at[i], zg_sem.at[i])
+        to_genes(place, place, zg_send_sem.at[n], zg_sem.at[n])
 
     @pl.loop(0, chunks)
     def _(i):
         slot = lax.rem(i, 3)
         load(i, slot).wait()
         here = block(i)
-
-        def tile(j, total):
-            lanes = block(j)
+        total = jnp.zeros((3 * BLOCK, TILE), F32)
+        total8 = jnp.zeros((2 * BLOCK, TILE), F32)
+        for j in range(tiles):
+            lanes = pl.ds(j * TILE, TILE)
             values = stage[slot, :, lanes] * mask_ref[i, j].astype(F32)
             top = values.astype(BF16)
-            rest = (values - top.astype(F32)).astype(BF16)
+            rest = ((values - top.astype(F32)) * LOW_SCALE).astype(FP8)
             high[here, lanes] = top
             low[here, lanes] = rest
-            return total + dot(start3[:, lanes], top, NT) + dot(start3[:, lanes], rest, NT)
-
-        total = lax.fori_loop(0, tiles, tile, jnp.zeros((3 * BLOCK, TILE), F32), unroll=UNROLL)
+            total = total + dot(start3[:, lanes], top, NT)
+            total8 = total8 + dot(start8[:, lanes], rest, NT)
 
         @pl.when(i + 3 < chunks)
         def _():
             load(i + 3, slot).start()
 
-        z_send[i] = fold3(total)
-        spread(i)
-
-        @pl.when(i > 0)
+        z_send[:, here] = fold3(total) + fold8(total8) * (1.0 / (64.0 * LOW_SCALE))
+
+        @pl.when(i == GROUPS[1][0] - 1)
         def _():
-            gather(i - 1)
+            spread(0)
+
+        @pl.when(i == chunks - 1)
+        def _():
+            spread(1)
+            gather(0)
 
     _, inverse0 = factor(take_gram(0))
 
     def side_of(step, inverse, full, first, count):
         lanes = pl.ds(first * TILE, count * TILE)
-        y3[step, pl.ds(0, 3 * BLOCK), lanes] = split3(small_product(inverse, full[:, lanes]))
-
-    def back(step, left_rows, first, count, lanes):
+        side = small_product(inverse, full[:, lanes])
+        top = largest([side])
+        y3[step, pl.ds(0, 3 * BLOCK), lanes] = split3(side)
+        y8[pl.ds(0, 2 * BLOCK), lanes] = pieces8(side, 256.0 / top)
+        return top * (1.0 / (256.0 * LOW_SCALE))
+
+    def back(step, undo, first, count, lanes):
         there = pl.ds(first * TILE, count * TILE)
-        left = y3[step, pl.ds(0, left_rows), there]
-        return dot(left, high[there, lanes], NN) + dot(left, low[there, lanes], NN)
+        extra = step == 0
+        product = dot(y3[step, pl.ds(0, 3 * BLOCK + 16 * extra), there], high[there, lanes], NN)
+        product8 = dot(y8[pl.ds(0, 2 * BLOCK + BLOCK * extra), there], low[there, lanes], NN)
+        part = fold3(product) + fold8(product8) * undo
+        if extra:
+            sums = product[3 * BLOCK : 3 * BLOCK + 8] + product8[2 * BLOCK : 2 * BLOCK + 8] * (1.0 / LOW_SCALE)
+            part = jnp.concatenate([part, sums], axis=0)
+        return part
 
     with_ones = 3 * BLOCK + 16
-    early, middle = EARLY, chunks - 1
-
-    def wait_chunks(first, last):
-        for i in range(first, last):
-            wait_bytes(z_recv.at[i, pl.ds(1, n_gene - 1)], zg_sem.at[i])
-
-    wait_chunks(0, early)
-    side_of(0, inverse0, z_full, 0, early)
-
-    @pl.loop(0, tiles // 2)
-    def _(t):
+    wait_bytes(z_recv.at[pl.ds(1, n_gene - 1)], zg_sem.at[0])
+    undo0 = side_of(0, inverse0, z_full, *GROUPS[0])
+
+    def early(t):
         lanes = block(t, 2 * TILE)
-        image_acc[:, lanes] = back(0, with_ones, 0, early, lanes)
-
-    gather(chunks - 1)
-    wait_chunks(early, middle)
-    side_of(0, inverse0, z_full, early, middle - early)
-
-    @pl.loop(0, tiles // 2)
-    def _(t):
-        lanes = block(t, 2 * TILE)
-        image_acc[:, lanes] += back(0, with_ones, early, middle - early, lanes)
-
+        image_acc[:, lanes] = back(0, undo0, *GROUPS[0], lanes)
+
+    pl.loop(0, 5)(early)
+    gather(1)
+    pl.loop(5, tiles // 2)(early)
     own = block(c)
     current = small_product(inverse0, start_ref[:, own])
     older = None
     inverse = inverse0
-    wait_chunks(middle, chunks)
-    side_of(0, inverse0, z_full, middle, chunks - middle)
+    wait_bytes(z_recv_b.at[pl.ds(1, n_gene - 1)], zg_sem.at[1])
+    undo = side_of(0, inverse0, z_full, *GROUPS[1])
     eye = lax.broadcasted_iota(jnp.int32, (BLOCK, BLOCK), 0) == lax.broadcasted_iota(jnp.int32, (BLOCK, BLOCK), 1)
     column_sums = None
     older_mean = None
@@ -336,11 +369,9 @@
             owner = cell_at(k, 1)
             lanes = block(owner)
             if step == 0:
-                product = image_acc[:, lanes] + back(0, with_ones, middle, chunks - middle, lanes)
-                sent[k, pl.ds(BLOCK, 8), :] = product[3 * BLOCK : 3 * BLOCK + 8]
+                sent[k] = image_acc[:, lanes] + back(0, undo, *GROUPS[1], lanes)
             else:
-                product = back(1, 3 * BLOCK, 0, chunks, lanes)
-            sent[k, pl.ds(0, BLOCK), :] = fold3(product)
+                sent[k] = back(1, undo, 0, chunks, lanes)
             return owner
 
         def send_image(k, owner):
@@ -389,26 +420,31 @@
             to_cells(place, place, ag_send_sem.at[step], lambda k: ag_sem.at[step, k])
             older_mean = mean_row
 
-            def multiply(lanes):
-                left = split3(resid[step, :, lanes])
-                resid3[:, lanes] = left
-                return dot(left, high[:, lanes], NT) + dot(left, low[:, lanes], NT)
-
             def arrived(k):
                 lanes = block(cell_at(k, -1))
                 wait_bytes(resid.at[step, :, lanes], ag_sem.at[step, k])
                 return lanes
 
-            acc[...] = multiply(own)
-
-            @pl.loop(0, n_cell // 2 - 1)
-            def _(t):
-                one = arrived(2 * t + 1)
-                two = arrived(2 * t + 2)
-                acc[...] += multiply(one) + multiply(two)
-
-            acc[...] += multiply(arrived(n_cell - 1))
-            z_send2[...] = fold3(acc)
+            for first, last in ((0, 5), (5, 11), (11, 16)):
+                lanes_of = [own if k == 0 else arrived(k) for k in range(first, last)]
+                values = [resid[step, :, lanes] for lanes in lanes_of]
+                top = largest(values)
+                for lanes, value in zip(lanes_of, values):
+                    resid3[:, lanes] = split3(value)
+                    resid8[:, lanes] = pieces8(value, 256.0 / top)
+                undo = top * (1.0 / (256.0 * LOW_SCALE))
+
+                @pl.loop(0, chunks // 2)
+                def _(i):
+                    for one in (2 * i, 2 * i + 1):
+                        there = block(one)
+                        total, total8 = 0.0, 0.0
+                        for lanes in lanes_of:
+                            total = total + dot(resid3[:, lanes], high[there, lanes], NT)
+                            total8 = total8 + dot(resid8[:, lanes], low[there, lanes], NT)
+                        total = fold3(total) + fold8(total8) * undo
+                        z_send2[:, there] = total if first == 0 else z_send2[:, there] + total
+
             half = rows // 2
 
             @pl.loop(1, n_gene)
@@ -439,7 +475,7 @@
             wait_bytes(parts, z2_sems.at[3])
             wait_bytes(parts, z2_sems.at[0])
             wait_bytes(parts, z2_sems.at[2])
-            side_of(1, inverse, z_full2, 0, chunks)
+            undo = side_of(1, inverse, z_full2, 0, chunks)
         else:
             last_buf[c] = pack(gram_of(split3(piece)))
             here = last_buf.at[c]
@@ -456,9 +492,9 @@
     for step in range(3):
         wait_bytes(gram_buf.at[step, pl.ds(0, n_gene - 1)], gram_sems.at[step, 0])
     wait_bytes(last_buf.at[pl.ds(0, n_cell - 1)], last_sems.at[0])
-    for i in range(chunks):
-        wait_bytes(z_recv.at[i, pl.ds(1, n_gene - 1)], z_send_sem.at[i])
-        wait_bytes(z_recv.at[i, pl.ds(1, n_gene - 1)], zg_send_sem.at[i])
+    for n in range(2):
+        wait_bytes(z_parts[n].at[pl.ds(1, n_gene - 1)], z_send_sem.at[n])
+        wait_bytes(z_parts[n].at[pl.ds(1, n_gene - 1)], zg_send_sem.at[n])
     for step in range(2):
         wait_bytes(stat_buf.at[step, pl.ds(0, n_cell - 1), pl.ds(0, 2 + step)], stat_send_sem.at[step])
         wait_bytes((i_recv if step == 0 else i_recv2).at[pl.ds(1, n_cell - 1)], rs_send_sem.at[step])
@@ -486,34 +522,37 @@
         out_specs=(vmem, vmem),
         scratch_shapes=[
             pltpu.VMEM((rows, width), BF16),
-            pltpu.VMEM((rows, width), BF16),
+            pltpu.VMEM((rows, width), FP8),
             pltpu.VMEM((3, TILE, width), F32),
             pltpu.VMEM((3 * BLOCK, width), BF16),
+            pltpu.VMEM((2 * BLOCK, width), FP8),
             pltpu.VMEM((3, n_gene, 8, 128), F32),
             pltpu.VMEM((n_cell, 8, 128), F32),
-            pltpu.VMEM((chunks, BLOCK, TILE), F32),
-            pltpu.VMEM((chunks, n_gene, 8, 128), F32),
+            pltpu.VMEM((BLOCK, rows), F32),
+            pltpu.VMEM((n_gene, 8, GROUPS[0][1] * 128), F32),
+            pltpu.VMEM((n_gene, 8, GROUPS[1][1] * 128), F32),
             pltpu.VMEM((BLOCK, rows), F32),
             pltpu.VMEM((BLOCK, rows), F32),
             pltpu.VMEM((n_gene, 8, rows // 2), F32),
             pltpu.VMEM((BLOCK, rows), F32),
             pltpu.VMEM((2, 3 * BLOCK + 16, rows), BF16),
+            pltpu.VMEM((3 * BLOCK, rows), FP8),
             pltpu.VMEM((2, n_cell, 3, 8, 128), F32),
-            pltpu.VMEM((3 * BLOCK + 16, width), F32),
+            pltpu.VMEM((BLOCK + 8, width), F32),
             pltpu.VMEM((n_cell, BLOCK + 8, TILE), F32),
             pltpu.VMEM((n_cell, BLOCK + 8, TILE), F32),
             pltpu.VMEM((n_cell, BLOCK, TILE), F32),
             pltpu.VMEM((n_cell, BLOCK, TILE), F32),
             pltpu.VMEM((2, BLOCK, width), F32),
             pltpu.VMEM((3 * BLOCK, width), BF16),
-            pltpu.VMEM((3 * BLOCK, rows), F32),
+            pltpu.VMEM((2 * BLOCK, width), FP8),
             dma((3,)),
             dma((3, 2)),
             dma((2,)),
-            dma((chunks,)),
-            dma((chunks,)),
-            dma((chunks,)),
-            dma((chunks,)),
+            dma((2,)),
+            dma((2,)),
+            dma((2,)),
+            dma((2,)),
             dma((4,)),
             dma((2,)),
             dma((2,)),

time: 104 us -> 93.8 us (0.902)
  Pallas kernels: 102 us -> 92.4 us
    pallas_call x1, Pallas kernels: 99.9 us -> 90 us  [per_device(): pl.pallas_call(functools.partial(kernel, sizes), out_shape=(jax.ShapeDtyp...]
where the time goes in v3:
time: 93.8 us; the launch traced here: 93 us
  Pallas kernels  92.4 us (99%)
    pallas_call x1, Pallas kernels, per_device(): pl.pallas_call(functools.partial(kernel, sizes), out_shape=(jax.ShapeDtyp...  90 us
    pallas_call x1, Pallas kernels, per_device(): pl.pallas_call(functools.partial(finish, math.sqrt(width * n_gene)), out_...  2.35 us

profile of v3, /device:TPU:1, one launch (start us, length us, event | category | flops | bytes accessed | tf_op | source)
XLA Modules:
  0.0 93.0 jit_solution(17053535035953869636)
XLA Ops:
  0.6 90.0 %lanczos.1 = (f32[5,32,32]{2,1,0:T(8,128)}, f32[32,4096]{1,0:T(8,128)}) custom-call(f32[1536,4096]{1,0:T(8,128)} %x_ref.1, s32[6,16]{1,0:T(8,128)} %mask_ref.1, f32[32,4096]{1,0:T(8,128)} %bitcast.2), custom_call_target="tpu_custom_call" | custom-call | tf_op jit(solution)/shard_map/lanczos/pallas_call | solution.py:515
  90.7 2.3 %finish.1 = (f32[2,32,32]{2,1,0:T(8,128)}, f32[2,32,32]{2,1,0:T(8,128)}, f32[32,4096]{1,0:T(8,128)}) custom-call(f32[5,32,32]{2,1,0:T(8,128)} %get-tuple-element.8.small_ref, f32[32,4096]{1,0:T(8,128)} %get-tuple-element.9.resid_ref), custom_call_target="tpu_custom_call" | custom-call | tf_op jit(solution)/shard_map/finish/pallas_call | solution.py:569

commit v4 on v3

--- a/solution.py
+++ b/solution.py
@@ -15,7 +15,7 @@
 BF16 = jnp.bfloat16
 FP8 = jnp.float8_e4m3fn
 LOW_SCALE = 4096.0
-GROUPS = ((0, 4), (4, 2))
+GROUPS = ((0, 3), (3, 3))
 
 NN = ((1,), (0,))
 NT = ((1,), (1,))
@@ -119,11 +119,7 @@
     last_buf,
     z_send,
     z_recv,
-    z_recv_b,
     z_full,
-    z_send2,
-    z_recv2,
-    z_full2,
     y3,
     y8,
     stat_buf,
@@ -142,13 +138,13 @@
     z_sem,
     zg_send_sem,
     zg_sem,
-    z2_sems,
     stat_send_sem,
     stat_sem,
     rs_send_sem,
     rs_sem,
     ag_send_sem,
     ag_sem,
+    out_sem,
 ):
     n_cell, n_gene, rows, width = sizes
     cells = rows * n_cell
@@ -203,10 +199,10 @@
                 device_id_type=MESH,
             ).start()
 
-    def to_cells(src, dst, send_sem, recv_sem_of):
+    def to_cells(src, dst, send_sem, recv_sem_of, near=False):
         @pl.loop(1, n_cell)
         def _(t):
-            k = n_cell - t
+            k = t if near else n_cell - t
             pltpu.make_async_remote_copy(
                 src_ref=src,
                 dst_ref=dst,
@@ -240,9 +236,7 @@
     pl.semaphore_wait(barrier, n_cell + n_gene - 2)
     send_gram(0, gram0)
 
-    z_parts = (z_recv, z_recv_b)
-
-    def spread(n):
+    def spread(step, n):
         first, count = GROUPS[n]
         half = count * 128
 
@@ -251,26 +245,29 @@
             peer = lax.rem(g + k, n_gene)
             pltpu.make_async_remote_copy(
                 src_ref=z_send.at[
-                    block(peer // 2, 8), pl.ds(pl.multiple_of(first * TILE + peer % 2 * half, 128), half)
+                    step, block(peer // 2, 8), pl.ds(pl.multiple_of(first * TILE + peer % 2 * half, 128), half)
                 ],
-                dst_ref=z_parts[n].at[k],
-                send_sem=z_send_sem.at[n],
-                recv_sem=z_sem.at[n],
+                dst_ref=z_recv.at[step, n, k],
+                send_sem=z_send_sem.at[step, n],
+                recv_sem=z_sem.at[step, n],
                 device_id=(c, peer),
                 device_id_type=MESH,
             ).start()
 
-    def gather(n):
+    def gather(step, n):
         first, count = GROUPS[n]
         half = count * 128
-        wait_bytes(z_parts[n].at[pl.ds(1, n_gene - 1)], z_sem.at[n])
-        there = (block(z, 8), pl.ds(pl.multiple_of(first * TILE + core * half, 128), half))
+        wait_bytes(z_recv.at[step, n, pl.ds(1, n_gene - 1)], z_sem.at[step, n])
+        there = (step, block(z, 8), pl.ds(pl.multiple_of(first * TILE + core * half, 128), half))
         total = z_send[there]
         for k in range(1, n_gene):
-            total = total + z_parts[n][k]
+            total = total + z_recv[step, n, k]
         place = z_full.at[there]
         place[...] = total
-        to_genes(place, place, zg_send_sem.at[n], zg_sem.at[n])
+        to_genes(place, place, zg_send_sem.at[step, n], zg_sem.at[step, n])
+
+    def gathered(step, n):
+        wait_bytes(z_recv.at[step, n, pl.ds(1, n_gene - 1)], zg_sem.at[step, n])
 
     @pl.loop(0, chunks)
     def _(i):
@@ -293,22 +290,25 @@
         def _():
             load(i + 3, slot).start()
 
-        z_send[:, here] = fold3(total) + fold8(total8) * (1.0 / (64.0 * LOW_SCALE))
+        z_send[0, :, here] = fold3(total) + fold8(total8) * (1.0 / (64.0 * LOW_SCALE))
 
         @pl.when(i == GROUPS[1][0] - 1)
         def _():
-            spread(0)
+            spread(0, 0)
+
+        @pl.when(i == chunks - 2)
+        def _():
+            gather(0, 0)
 
         @pl.when(i == chunks - 1)
         def _():
-            spread(1)
-            gather(0)
+            spread(0, 1)
 
     _, inverse0 = factor(take_gram(0))
 
-    def side_of(step, inverse, full, first, count):
+    def side_of(step, inverse, first, count):
         lanes = pl.ds(first * TILE, count * TILE)
-        side = small_product(inverse, full[:, lanes])
+        side = small_product(inverse, z_full[step, :, lanes])
         top = largest([side])
         y3[step, pl.ds(0, 3 * BLOCK), lanes] = split3(side)
         y8[pl.ds(0, 2 * BLOCK), lanes] = pieces8(side, 256.0 / top)
@@ -326,41 +326,42 @@
         return part
 
     with_ones = 3 * BLOCK + 16
-    wait_bytes(z_recv.at[pl.ds(1, n_gene - 1)], zg_sem.at[0])
-    undo0 = side_of(0, inverse0, z_full, *GROUPS[0])
+    gathered(0, 0)
+    undo0 = side_of(0, inverse0, *GROUPS[0])
 
     def early(t):
         lanes = block(t, 2 * TILE)
         image_acc[:, lanes] = back(0, undo0, *GROUPS[0], lanes)
 
     pl.loop(0, 5)(early)
-    gather(1)
+    gather(0, 1)
     pl.loop(5, tiles // 2)(early)
     own = block(c)
     current = small_product(inverse0, start_ref[:, own])
     older = None
     inverse = inverse0
-    wait_bytes(z_recv_b.at[pl.ds(1, n_gene - 1)], zg_sem.at[1])
-    undo = side_of(0, inverse0, z_full, *GROUPS[1])
+    gathered(0, 1)
+    undo = side_of(0, inverse0, *GROUPS[1])
     eye = lax.broadcasted_iota(jnp.int32, (BLOCK, BLOCK), 0) == lax.broadcasted_iota(jnp.int32, (BLOCK, BLOCK), 1)
     column_sums = None
     older_mean = None
 
     for step in range(2):
-        if step == 0:
-            stat = dot(y3[0], y3[0], NT)
-        else:
-            stat = dot(y3[1], jnp.concatenate([y3[1], y3[0]], axis=0), NT)
-        row = fold_lanes(stat[3 * BLOCK : 3 * BLOCK + 8])
-        stat = fold3(stat)
-        stat_buf[step, c, 0] = pack(fold_lanes(stat))
-        stat_buf[step, c, 1] = jnp.concatenate([row, jnp.zeros((8, 128 - BLOCK), F32)], axis=1)
-        count = 2
-        if step == 1:
-            stat_buf[step, c, 2] = pack(fold_lanes(stat, with_ones))
-            count = 3
-        here = stat_buf.at[step, c, pl.ds(0, count)]
-        to_cells(here, here, stat_send_sem.at[step], lambda k: stat_sem.at[step])
+        count = 2 + step
+
+        def send_stat():
+            if step == 0:
+                stat = dot(y3[0], y3[0], NT)
+            else:
+                stat = dot(y3[1], jnp.concatenate([y3[1], y3[0]], axis=0), NT)
+            row = fold_lanes(stat[3 * BLOCK : 3 * BLOCK + 8])
+            stat = fold3(stat)
+            stat_buf[step, c, 0] = pack(fold_lanes(stat))
+            stat_buf[step, c, 1] = jnp.concatenate([row, jnp.zeros((8, 128 - BLOCK), F32)], axis=1)
+            if step == 1:
+                stat_buf[step, c, 2] = pack(fold_lanes(stat, with_ones))
+            here = stat_buf.at[step, c, pl.ds(0, count)]
+            to_cells(here, here, stat_send_sem.at[step], lambda k: stat_sem.at[step])
 
         sent = i_send if step == 0 else i_send2
         got = i_recv if step == 0 else i_recv2
@@ -394,6 +395,8 @@
             @pl.when(t < n_cell // 2 - 1)
             def _():
                 send_image(two, owner_two)
+
+            pl.when(t == 1)(send_stat)
 
         wait_bytes(stat_buf.at[step, pl.ds(0, n_cell - 1), pl.ds(0, count)], stat_sem.at[step])
         stats = [sum_slots(stat_buf.at[step, :, k], n_cell) / cells for k in range(count)]
@@ -417,7 +420,7 @@
         place[...] = piece
 
         if step == 0:
-            to_cells(place, place, ag_send_sem.at[step], lambda k: ag_sem.at[step, k])
+            to_cells(place, place, ag_send_sem.at[step], lambda k: ag_sem.at[step, k], True)
             older_mean = mean_row
 
             def arrived(k):
@@ -434,48 +437,30 @@
                     resid8[:, lanes] = pieces8(value, 256.0 / top)
                 undo = top * (1.0 / (256.0 * LOW_SCALE))
 
-                @pl.loop(0, chunks // 2)
+                @pl.loop(0, 2)
                 def _(i):
-                    for one in (2 * i, 2 * i + 1):
+                    for one in (3 * i, 3 * i + 1, 3 * i + 2):
                         there = block(one)
                         total, total8 = 0.0, 0.0
                         for lanes in lanes_of:
                             total = total + dot(resid3[:, lanes], high[there, lanes], NT)
                             total8 = total8 + dot(resid8[:, lanes], low[there, lanes], NT)
                         total = fold3(total) + fold8(total8) * undo
-                        z_send2[:, there] = total if first == 0 else z_send2[:, there] + total
-
-            half = rows // 2
-
-            @pl.loop(1, n_gene)
-            def _(k):
-                peer = lax.rem(g + k, n_gene)
-                pltpu.make_async_remote_copy(
-                    src_ref=z_send2.at[block(peer // 2, 8), block(peer % 2, half)],
-                    dst_ref=z_recv2.at[k],
-                    send_sem=z2_sems.at[0],
-                    recv_sem=z2_sems.at[1],
-                    device_id=(c, peer),
-                    device_id_type=MESH,
-                ).start()
+                        z_send[1, :, there] = total if first == 0 else z_send[1, :, there] + total
+                    if last == n_cell:
+                        for n in range(2):
+                            pl.when(i == n)(functools.partial(spread, 1, n))
 
             send_gram(1, pack(gram_of(resid3[...])))
-            parts = z_recv2.at[pl.ds(1, n_gene - 1)]
-            wait_bytes(parts, z2_sems.at[1])
-            total = z_send2[block(z, 8), block(core, half)]
-            for k in range(1, n_gene):
-                total = total + z_recv2[k]
-            place = z_full2.at[block(z, 8), block(core, half)]
-            place[...] = total
-            to_genes(place, place, z2_sems.at[2], z2_sems.at[3])
+            gather(1, 0)
+            gather(1, 1)
             upper, inverse = factor(take_gram(1))
             small_ref[3] = upper
             older = current
             current = small_product(inverse, piece)
-            wait_bytes(parts, z2_sems.at[3])
-            wait_bytes(parts, z2_sems.at[0])
-            wait_bytes(parts, z2_sems.at[2])
-            undo = side_of(1, inverse, z_full2, 0, chunks)
+            gathered(1, 0)
+            gathered(1, 1)
+            undo = side_of(1, inverse, 0, chunks)
         else:
             last_buf[c] = pack(gram_of(split3(piece)))
             here = last_buf.at[c]
@@ -484,18 +469,19 @@
             wait_bytes(last_buf.at[pl.ds(0, n_cell - 1)], last_sems.at[1])
             send_gram(2, sum_slots(last_buf, n_cell))
             wait_bytes(resid.at[step, :, pl.ds(0, (n_cell - 1) * TILE)], ag_sem.at[step, 0])
-            resid_ref[...] = resid[step]
+            pltpu.make_async_copy(resid.at[step], resid_ref, out_sem).start()
             upper, inverse = factor(take_gram(2))
             small_ref[0] = inverse
             small_ref[4] = upper
+            pltpu.make_async_copy(resid.at[step], resid_ref, out_sem).wait()
 
     for step in range(3):
         wait_bytes(gram_buf.at[step, pl.ds(0, n_gene - 1)], gram_sems.at[step, 0])
     wait_bytes(last_buf.at[pl.ds(0, n_cell - 1)], last_sems.at[0])
-    for n in range(2):
-        wait_bytes(z_parts[n].at[pl.ds(1, n_gene - 1)], z_send_sem.at[n])
-        wait_bytes(z_parts[n].at[pl.ds(1, n_gene - 1)], zg_send_sem.at[n])
     for step in range(2):
+        for n in range(2):
+            wait_bytes(z_recv.at[step, n, pl.ds(1, n_gene - 1)], z_send_sem.at[step, n])
+            wait_bytes(z_recv.at[step, n, pl.ds(1, n_gene - 1)], zg_send_sem.at[step, n])
         wait_bytes(stat_buf.at[step, pl.ds(0, n_cell - 1), pl.ds(0, 2 + step)], stat_send_sem.at[step])
         wait_bytes((i_recv if step == 0 else i_recv2).at[pl.ds(1, n_cell - 1)], rs_send_sem.at[step])
         wait_bytes(resid.at[step, :, pl.ds(0, (n_cell - 1) * TILE)], ag_send_sem.at[step])
@@ -519,7 +505,7 @@
             jax.ShapeDtypeStruct((BLOCK, width), F32),
         ),
         in_specs=[pl.BlockSpec(memory_space=pl.ANY), pl.BlockSpec(memory_space=pltpu.SMEM), vmem],
-        out_specs=(vmem, vmem),
+        out_specs=(vmem, pl.BlockSpec(memory_space=pl.ANY)),
         scratch_shapes=[
             pltpu.VMEM((rows, width), BF16),
             pltpu.VMEM((rows, width), FP8),
@@ -528,13 +514,9 @@
             pltpu.VMEM((2 * BLOCK, width), FP8),
             pltpu.VMEM((3, n_gene, 8, 128), F32),
             pltpu.VMEM((n_cell, 8, 128), F32),
-            pltpu.VMEM((BLOCK, rows), F32),
-            pltpu.VMEM((n_gene, 8, GROUPS[0][1] * 128), F32),
-            pltpu.VMEM((n_gene, 8, GROUPS[1][1] * 128), F32),
-            pltpu.VMEM((BLOCK, rows), F32),
-            pltpu.VMEM((BLOCK, rows), F32),
-            pltpu.VMEM((n_gene, 8, rows // 2), F32),
-            pltpu.VMEM((BLOCK, rows), F32),
+            pltpu.VMEM((2, BLOCK, rows), F32),
+            pltpu.VMEM((2, 2, n_gene, 8, GROUPS[0][1] * 128), F32),
+            pltpu.VMEM((2, BLOCK, rows), F32),
             pltpu.VMEM((2, 3 * BLOCK + 16, rows), BF16),
             pltpu.VMEM((3 * BLOCK, rows), FP8),
             pltpu.VMEM((2, n_cell, 3, 8, 128), F32),
@@ -549,17 +531,17 @@
             dma((3,)),
             dma((3, 2)),
             dma((2,)),
-            dma((2,)),
-            dma((2,)),
-            dma((2,)),
-            dma((2,)),
-            dma((4,)),
+            dma((2, 2)),
+            dma((2, 2)),
+            dma((2, 2)),
+            dma((2, 2)),
             dma((2,)),
             dma((2,)),
             dma((2,)),
             dma((2,)),
             dma((2,)),
             dma((2, n_cell)),
+            dma,
         ],
         compiler_params=pltpu.CompilerParams(
             collective_id=0, has_side_effects=True, vmem_limit_bytes=60 * 2**20

time: 93.8 us -> 88.1 us (0.939)
  Pallas kernels: 92.4 us -> 87.3 us
    pallas_call x1, Pallas kernels: 90 us -> 84.9 us  [per_device(): pl.pallas_call(functools.partial(kernel, sizes), out_shape=(jax.ShapeDtyp...]
where the time goes in v4:
time: 88.1 us; the launch traced here: 87.9 us
  Pallas kernels  87.3 us (99%)
    pallas_call x1, Pallas kernels, per_device(): pl.pallas_call(functools.partial(kernel, sizes), out_shape=(jax.ShapeDtyp...  84.9 us
    pallas_call x1, Pallas kernels, per_device(): pl.pallas_call(functools.partial(finish, math.sqrt(width * n_gene)), out_...  2.35 us

profile of v4, /device:TPU:1, one launch (start us, length us, event | category | flops | bytes accessed | tf_op | source)
XLA Modules:
  0.0 87.9 jit_solution(616824541811702664)
XLA Ops:
  0.6 84.9 %lanczos.1 = (f32[5,32,32]{2,1,0:T(8,128)}, f32[32,4096]{1,0:T(8,128)}) custom-call(f32[1536,4096]{1,0:T(8,128)} %x_ref.1, s32[6,16]{1,0:T(8,128)} %mask_ref.1, f32[32,4096]{1,0:T(8,128)} %bitcast.2), custom_call_target="tpu_custom_call" | custom-call | tf_op jit(solution)/shard_map/lanczos/pallas_call | solution.py:501
  85.6 2.3 %finish.1 = (f32[2,32,32]{2,1,0:T(8,128)}, f32[2,32,32]{2,1,0:T(8,128)}, f32[32,4096]{1,0:T(8,128)}) custom-call(f32[5,32,32]{2,1,0:T(8,128)} %get-tuple-element.8.small_ref, f32[32,4096]{1,0:T(8,128)} %get-tuple-element.9.resid_ref), custom_call_target="tpu_custom_call" | custom-call | tf_op jit(solution)/shard_map/finish/pallas_call | solution.py:551

commit v5 on v4

--- a/solution.py
+++ b/solution.py
@@ -229,12 +229,9 @@
 
     start3[...] = split3(start_ref[...])
     start8[...] = pieces8(start_ref[...], 64.0)
-    gram0 = pack(gram_of(start3[...]))
     y3[0, pl.ds(3 * BLOCK, 16), :] = jnp.ones((16, rows), BF16)
     y3[1, pl.ds(3 * BLOCK, 16), :] = jnp.ones((16, rows), BF16)
     y8[pl.ds(2 * BLOCK, BLOCK), :] = jnp.ones((BLOCK, rows), FP8)
-    pl.semaphore_wait(barrier, n_cell + n_gene - 2)
-    send_gram(0, gram0)
 
     def spread(step, n):
         first, count = GROUPS[n]
@@ -290,21 +287,25 @@
         def _():
             load(i + 3, slot).start()
 
+        @pl.when(i == 1)
+        def _():
+            pl.semaphore_wait(barrier, n_cell + n_gene - 2)
+            send_gram(0, pack(gram_of(start3[...])))
+
         z_send[0, :, here] = fold3(total) + fold8(total8) * (1.0 / (64.0 * LOW_SCALE))
 
         @pl.when(i == GROUPS[1][0] - 1)
         def _():
             spread(0, 0)
 
-        @pl.when(i == chunks - 2)
-        def _():
-            gather(0, 0)
-
         @pl.when(i == chunks - 1)
         def _():
             spread(0, 1)
+            gather(0, 0)
 
     _, inverse0 = factor(take_gram(0))
+    current = small_product(inverse0, start_ref[:, block(c)])
+    gather(0, 1)
 
     def side_of(step, inverse, first, count):
         lanes = pl.ds(first * TILE, count * TILE)
@@ -333,11 +334,8 @@
         lanes = block(t, 2 * TILE)
         image_acc[:, lanes] = back(0, undo0, *GROUPS[0], lanes)
 
-    pl.loop(0, 5)(early)
-    gather(0, 1)
-    pl.loop(5, tiles // 2)(early)
+    pl.loop(0, tiles // 2)(early)
     own = block(c)
-    current = small_product(inverse0, start_ref[:, own])
     older = None
     inverse = inverse0
     gathered(0, 1)

time: 88.1 us -> 85.4 us (0.969)
  Pallas kernels: 87.3 us -> 84.2 us
    pallas_call x1, Pallas kernels: 84.9 us -> 81.8 us  [per_device(): pl.pallas_call(functools.partial(kernel, sizes), out_shape=(jax.ShapeDtyp...]
where the time goes in v5:
time: 85.4 us; the launch traced here: 84.8 us
  Pallas kernels  84.2 us (99%)
    pallas_call x1, Pallas kernels, per_device(): pl.pallas_call(functools.partial(kernel, sizes), out_shape=(jax.ShapeDtyp...  81.8 us
    pallas_call x1, Pallas kernels, per_device(): pl.pallas_call(functools.partial(finish, math.sqrt(width * n_gene)), out_...  2.35 us

profile of v5, /device:TPU:1, one launch (start us, length us, event | category | flops | bytes accessed | tf_op | source)
XLA Modules:
  0.0 84.8 jit_solution(9225870757073134174)
XLA Ops:
  0.6 81.8 %lanczos.1 = (f32[5,32,32]{2,1,0:T(8,128)}, f32[32,4096]{1,0:T(8,128)}) custom-call(f32[1536,4096]{1,0:T(8,128)} %x_ref.1, s32[6,16]{1,0:T(8,128)} %mask_ref.1, f32[32,4096]{1,0:T(8,128)} %bitcast.2), custom_call_target="tpu_custom_call" | custom-call | tf_op jit(solution)/shard_map/lanczos/pallas_call | solution.py:499
  82.5 2.3 %finish.1 = (f32[2,32,32]{2,1,0:T(8,128)}, f32[2,32,32]{2,1,0:T(8,128)}, f32[32,4096]{1,0:T(8,128)}) custom-call(f32[5,32,32]{2,1,0:T(8,128)} %get-tuple-element.8.small_ref, f32[32,4096]{1,0:T(8,128)} %get-tuple-element.9.resid_ref), custom_call_target="tpu_custom_call" | custom-call | tf_op jit(solution)/shard_map/finish/pallas_call | solution.py:549

commit v6 on v5

--- a/solution.py
+++ b/solution.py
@@ -15,6 +15,7 @@
 BF16 = jnp.bfloat16
 FP8 = jnp.float8_e4m3fn
 LOW_SCALE = 4096.0
+PIVOTS = 8
 GROUPS = ((0, 3), (3, 3))
 
 NN = ((1,), (0,))
@@ -92,11 +93,14 @@
     lane_of = lax.broadcasted_iota(jnp.int32, (BLOCK, 128), 1)
     both = jnp.concatenate([gram, jnp.zeros((BLOCK, 128 - BLOCK), F32)], axis=1)
     both = both + (lane_of == row_of + BLOCK).astype(F32)
-    for k in range(BLOCK - 1):
-        row = both[k : k + 1, :]
-        scaled = row / row[:, k : k + 1]
-        column = jnp.where(row_of[:, 0:1] > k, both[:, k : k + 1], 0.0)
-        both = both - column * scaled
+    for first in range(0, BLOCK, PIVOTS):
+        columns = [jnp.broadcast_to(both[:, first + p : first + p + 1], (BLOCK, 128)) for p in range(PIVOTS)]
+        for p in range(PIVOTS):
+            at = first + p
+            factors = jnp.where(row_of > at, columns[p] * (1.0 / columns[p][at : at + 1, :]), 0.0)
+            for q in range(p + 1, PIVOTS):
+                columns[q] = columns[q] - factors * columns[q][at : at + 1, :]
+            both = both - factors * both[at : at + 1, :]
     diagonal = jnp.sum(jnp.where(lane_of == row_of, both, 0.0), axis=1, keepdims=True)
     both = both / jnp.sqrt(diagonal)
     upper = jnp.where(lane_of >= row_of, both, 0.0)
@@ -126,8 +130,8 @@
     image_acc,
     i_send,
     i_recv,
-    i_send2,
-    i_recv2,
+    column_part,
+    column_recv,
     resid,
     resid3,
     resid8,
@@ -145,6 +149,7 @@
     ag_send_sem,
     ag_sem,
     out_sem,
+    column_sems,
 ):
     n_cell, n_gene, rows, width = sizes
     cells = rows * n_cell
@@ -231,7 +236,7 @@
     start8[...] = pieces8(start_ref[...], 64.0)
     y3[0, pl.ds(3 * BLOCK, 16), :] = jnp.ones((16, rows), BF16)
     y3[1, pl.ds(3 * BLOCK, 16), :] = jnp.ones((16, rows), BF16)
-    y8[pl.ds(2 * BLOCK, BLOCK), :] = jnp.ones((BLOCK, rows), FP8)
+    column_part[...] = jnp.zeros((8, width), F32)
 
     def spread(step, n):
         first, count = GROUPS[n]
@@ -278,6 +283,7 @@
             values = stage[slot, :, lanes] * mask_ref[i, j].astype(F32)
             top = values.astype(BF16)
             rest = ((values - top.astype(F32)) * LOW_SCALE).astype(FP8)
+            column_part[:, lanes] += jnp.sum(values.reshape(TILE // 8, 8, TILE), axis=0)
             high[here, lanes] = top
             low[here, lanes] = rest
             total = total + dot(start3[:, lanes], top, NT)
@@ -306,25 +312,33 @@
     _, inverse0 = factor(take_gram(0))
     current = small_product(inverse0, start_ref[:, block(c)])
     gather(0, 1)
+
+    @pl.loop(1, n_cell)
+    def _(k):
+        owner = cell_at(k, 1)
+        pltpu.make_async_remote_copy(
+            src_ref=column_part.at[:, block(owner)],
+            dst_ref=column_recv.at[k],
+            send_sem=column_sems.at[0],
+            recv_sem=column_sems.at[1],
+            device_id=(owner, g),
+            device_id_type=MESH,
+        ).start()
+
 
     def side_of(step, inverse, first, count):
         lanes = pl.ds(first * TILE, count * TILE)
         side = small_product(inverse, z_full[step, :, lanes])
         top = largest([side])
         y3[step, pl.ds(0, 3 * BLOCK), lanes] = split3(side)
-        y8[pl.ds(0, 2 * BLOCK), lanes] = pieces8(side, 256.0 / top)
+        y8[:, lanes] = pieces8(side, 256.0 / top)
         return top * (1.0 / (256.0 * LOW_SCALE))
 
     def back(step, undo, first, count, lanes):
         there = pl.ds(first * TILE, count * TILE)
-        extra = step == 0
-        product = dot(y3[step, pl.ds(0, 3 * BLOCK + 16 * extra), there], high[there, lanes], NN)
-        product8 = dot(y8[pl.ds(0, 2 * BLOCK + BLOCK * extra), there], low[there, lanes], NN)
-        part = fold3(product) + fold8(product8) * undo
-        if extra:
-            sums = product[3 * BLOCK : 3 * BLOCK + 8] + product8[2 * BLOCK : 2 * BLOCK + 8] * (1.0 / LOW_SCALE)
-            part = jnp.concatenate([part, sums], axis=0)
-        return part
+        product = dot(y3[step, pl.ds(0, 3 * BLOCK), there], high[there, lanes], NN)
+        product8 = dot(y8[:, there], low[there, lanes], NN)
+        return fold3(product) + fold8(product8) * undo
 
     with_ones = 3 * BLOCK + 16
     gathered(0, 0)
@@ -336,12 +350,12 @@
 
     pl.loop(0, tiles // 2)(early)
     own = block(c)
+    column_sums = None
     older = None
     inverse = inverse0
     gathered(0, 1)
     undo = side_of(0, inverse0, *GROUPS[1])
     eye = lax.broadcasted_iota(jnp.int32, (BLOCK, BLOCK), 0) == lax.broadcasted_iota(jnp.int32, (BLOCK, BLOCK), 1)
-    column_sums = None
     older_mean = None
 
     for step in range(2):
@@ -361,8 +375,7 @@
             here = stat_buf.at[step, c, pl.ds(0, count)]
             to_cells(here, here, stat_send_sem.at[step], lambda k: stat_sem.at[step])
 
-        sent = i_send if step == 0 else i_send2
-        got = i_recv if step == 0 else i_recv2
+        sent, got = i_send.at[step], i_recv.at[step]
 
         def image(k):
             owner = cell_at(k, 1)
@@ -396,6 +409,13 @@
 
             pl.when(t == 1)(send_stat)
 
+        if step == 0:
+            wait_bytes(column_recv.at[pl.ds(1, n_cell - 1)], column_sems.at[1])
+            column_sums = column_part[:, own]
+            for k in range(1, n_cell):
+                column_sums = column_sums + column_recv[k]
+            column_sums = jnp.sum(column_sums, axis=0, keepdims=True)
+
         wait_bytes(stat_buf.at[step, pl.ds(0, n_cell - 1), pl.ds(0, count)], stat_sem.at[step])
         stats = [sum_slots(stat_buf.at[step, :, k], n_cell) / cells for k in range(count)]
         mean_row = stats[1][0:1, 0:BLOCK]
@@ -407,9 +427,7 @@
         piece = sent[0]
         for k in range(1, n_cell):
             piece = piece + got[k]
-        if step == 0:
-            column_sums = piece[BLOCK : BLOCK + 1]
-        piece = (piece[0:BLOCK] - mean_column * column_sums) / cells
+        piece = (piece - mean_column * column_sums) / cells
         piece = piece - small_product(alpha, current)
         if step > 0:
             prior = unpack(stats[2]) - mean_column * older_mean
@@ -473,6 +491,7 @@
             small_ref[4] = upper
             pltpu.make_async_copy(resid.at[step], resid_ref, out_sem).wait()
 
+    wait_bytes(column_recv.at[pl.ds(1, n_cell - 1)], column_sems.at[0])
     for step in range(3):
         wait_bytes(gram_buf.at[step, pl.ds(0, n_gene - 1)], gram_sems.at[step, 0])
     wait_bytes(last_buf.at[pl.ds(0, n_cell - 1)], last_sems.at[0])
@@ -481,7 +500,7 @@
             wait_bytes(z_recv.at[step, n, pl.ds(1, n_gene - 1)], z_send_sem.at[step, n])
             wait_bytes(z_recv.at[step, n, pl.ds(1, n_gene - 1)], zg_send_sem.at[step, n])
         wait_bytes(stat_buf.at[step, pl.ds(0, n_cell - 1), pl.ds(0, 2 + step)], stat_send_sem.at[step])
-        wait_bytes((i_recv if step == 0 else i_recv2).at[pl.ds(1, n_cell - 1)], rs_send_sem.at[step])
+        wait_bytes(i_recv.at[step, pl.ds(1, n_cell - 1)], rs_send_sem.at[step])
         wait_bytes(resid.at[step, :, pl.ds(0, (n_cell - 1) * TILE)], ag_send_sem.at[step])
 
 
@@ -516,13 +535,13 @@
             pltpu.VMEM((2, 2, n_gene, 8, GROUPS[0][1] * 128), F32),
             pltpu.VMEM((2, BLOCK, rows), F32),
             pltpu.VMEM((2, 3 * BLOCK + 16, rows), BF16),
-            pltpu.VMEM((3 * BLOCK, rows), FP8),
+            pltpu.VMEM((2 * BLOCK, rows), FP8),
             pltpu.VMEM((2, n_cell, 3, 8, 128), F32),
-            pltpu.VMEM((BLOCK + 8, width), F32),
-            pltpu.VMEM((n_cell, BLOCK + 8, TILE), F32),
-            pltpu.VMEM((n_cell, BLOCK + 8, TILE), F32),
-            pltpu.VMEM((n_cell, BLOCK, TILE), F32),
-            pltpu.VMEM((n_cell, BLOCK, TILE), F32),
+            pltpu.VMEM((BLOCK, width), F32),
+            pltpu.VMEM((2, n_cell, BLOCK, TILE), F32),
+            pltpu.VMEM((2, n_cell, BLOCK, TILE), F32),
+            pltpu.VMEM((8, width), F32),
+            pltpu.VMEM((n_cell, 8, TILE), F32),
             pltpu.VMEM((2, BLOCK, width), F32),
             pltpu.VMEM((3 * BLOCK, width), BF16),
             pltpu.VMEM((2 * BLOCK, width), FP8),
@@ -540,6 +559,7 @@
             dma((2,)),
             dma((2, n_cell)),
             dma,
+            dma((2,)),
         ],
         compiler_params=pltpu.CompilerParams(
             collective_id=0, has_side_effects=True, vmem_limit_bytes=60 * 2**20

time: 85.4 us -> 82.5 us (0.966)
  Pallas kernels: 84.2 us -> 81.6 us
    pallas_call x1, Pallas kernels: 81.8 us -> 79.2 us  [per_device(): pl.pallas_call(functools.partial(kernel, sizes), out_shape=(jax.ShapeDtyp...]
where the time goes in v6:
time: 82.5 us; the launch traced here: 82.2 us
  Pallas kernels  81.6 us (99%)
    pallas_call x1, Pallas kernels, per_device(): pl.pallas_call(functools.partial(kernel, sizes), out_shape=(jax.ShapeDtyp...  79.2 us
    pallas_call x1, Pallas kernels, per_device(): pl.pallas_call(functools.partial(finish, math.sqrt(width * n_gene)), out_...  2.35 us

profile of v6, /device:TPU:1, one launch (start us, length us, event | category | flops | bytes accessed | tf_op | source)
XLA Modules:
  0.0 82.2 jit_solution(15771560062333732378)
XLA Ops:
  0.6 79.2 %lanczos.1 = (f32[5,32,32]{2,1,0:T(8,128)}, f32[32,4096]{1,0:T(8,128)}) custom-call(f32[1536,4096]{1,0:T(8,128)} %x_ref.1, s32[6,16]{1,0:T(8,128)} %mask_ref.1, f32[32,4096]{1,0:T(8,128)} %bitcast.2), custom_call_target="tpu_custom_call" | custom-call | tf_op jit(solution)/shard_map/lanczos/pallas_call | solution.py:518
  79.9 2.3 %finish.1 = (f32[2,32,32]{2,1,0:T(8,128)}, f32[2,32,32]{2,1,0:T(8,128)}, f32[32,4096]{1,0:T(8,128)}) custom-call(f32[5,32,32]{2,1,0:T(8,128)} %get-tuple-element.8.small_ref, f32[32,4096]{1,0:T(8,128)} %get-tuple-element.9.resid_ref), custom_call_target="tpu_custom_call" | custom-call | tf_op jit(solution)/shard_map/finish/pallas_call | solution.py:569

commit v7 on v6

--- a/solution.py
+++ b/solution.py
@@ -132,6 +132,7 @@
     i_recv,
     column_part,
     column_recv,
+    taken_ref,
     resid,
     resid3,
     resid8,
@@ -205,8 +206,7 @@
             ).start()
 
     def to_cells(src, dst, send_sem, recv_sem_of, near=False):
-        @pl.loop(1, n_cell)
-        def _(t):
+        for t in range(1, n_cell):
             k = t if near else n_cell - t
             pltpu.make_async_remote_copy(
                 src_ref=src,
@@ -423,15 +423,17 @@
         alpha = unpack(stats[0]) - mean_column * mean_row
         small_ref[1 + step] = alpha
 
+        taken = small_product(alpha, current)
+        if step > 0:
+            prior = unpack(stats[2]) - mean_column * older_mean
+            taken = taken + small_product(prior, older)
+        taken_ref[...] = mean_column * column_sums + taken * cells
+
         wait_bytes(got.at[pl.ds(1, n_cell - 1)], rs_sem.at[step])
         piece = sent[0]
         for k in range(1, n_cell):
             piece = piece + got[k]
-        piece = (piece - mean_column * column_sums) / cells
-        piece = piece - small_product(alpha, current)
-        if step > 0:
-            prior = unpack(stats[2]) - mean_column * older_mean
-            piece = piece - small_product(prior, older)
+        piece = (piece - taken_ref[...]) * (1.0 / cells)
         place = resid.at[step, :, own]
         place[...] = piece
 
@@ -482,6 +484,17 @@
             here = last_buf.at[c]
             to_cells(here, here, last_sems.at[0], lambda k: last_sems.at[1])
             to_cells(place, place, ag_send_sem.at[step], lambda k: ag_sem.at[step, 0])
+
+            wait_bytes(column_recv.at[pl.ds(1, n_cell - 1)], column_sems.at[0])
+            for k in range(2):
+                wait_bytes(gram_buf.at[k, pl.ds(0, n_gene - 1)], gram_sems.at[k, 0])
+                for n in range(2):
+                    wait_bytes(z_recv.at[k, n, pl.ds(1, n_gene - 1)], z_send_sem.at[k, n])
+                    wait_bytes(z_recv.at[k, n, pl.ds(1, n_gene - 1)], zg_send_sem.at[k, n])
+                wait_bytes(stat_buf.at[k, pl.ds(0, n_cell - 1), pl.ds(0, 2 + k)], stat_send_sem.at[k])
+                wait_bytes(i_recv.at[k, pl.ds(1, n_cell - 1)], rs_send_sem.at[k])
+            wait_bytes(resid.at[0, :, pl.ds(0, (n_cell - 1) * TILE)], ag_send_sem.at[0])
+
             wait_bytes(last_buf.at[pl.ds(0, n_cell - 1)], last_sems.at[1])
             send_gram(2, sum_slots(last_buf, n_cell))
             wait_bytes(resid.at[step, :, pl.ds(0, (n_cell - 1) * TILE)], ag_sem.at[step, 0])
@@ -491,17 +504,12 @@
             small_ref[4] = upper
             pltpu.make_async_copy(resid.at[step], resid_ref, out_sem).wait()
 
-    wait_bytes(column_recv.at[pl.ds(1, n_cell - 1)], column_sems.at[0])
-    for step in range(3):
-        wait_bytes(gram_buf.at[step, pl.ds(0, n_gene - 1)], gram_sems.at[step, 0])
-    wait_bytes(last_buf.at[pl.ds(0, n_cell - 1)], last_sems.at[0])
-    for step in range(2):
-        for n in range(2):
-            wait_bytes(z_recv.at[step, n, pl.ds(1, n_gene - 1)], z_send_sem.at[step, n])
-            wait_bytes(z_recv.at[step, n, pl.ds(1, n_gene - 1)], zg_send_sem.at[step, n])
-        wait_bytes(stat_buf.at[step, pl.ds(0, n_cell - 1), pl.ds(0, 2 + step)], stat_send_sem.at[step])
-        wait_bytes(i_recv.at[step, pl.ds(1, n_cell - 1)], rs_send_sem.at[step])
-        wait_bytes(resid.at[step, :, pl.ds(0, (n_cell - 1) * TILE)], ag_send_sem.at[step])
+    for sem, part in (
+        (gram_sems.at[2, 0], gram_buf.at[2, pl.ds(0, n_gene - 1)]),
+        (last_sems.at[0], last_buf.at[pl.ds(0, n_cell - 1)]),
+        (ag_send_sem.at[1], resid.at[1, :, pl.ds(0, (n_cell - 1) * TILE)]),
+    ):
+        wait_bytes(part, sem)
 
 
 def finish(scale, small_ref, resid_ref, alphas_ref, betas_ref, next_ref):
@@ -542,6 +550,7 @@
             pltpu.VMEM((2, n_cell, BLOCK, TILE), F32),
             pltpu.VMEM((8, width), F32),
             pltpu.VMEM((n_cell, 8, TILE), F32),
+            pltpu.VMEM((BLOCK, TILE), F32),
             pltpu.VMEM((2, BLOCK, width), F32),
             pltpu.VMEM((3 * BLOCK, width), BF16),
             pltpu.VMEM((2 * BLOCK, width), FP8),

time: 82.5 us -> 82 us (level)
  no operation moved by 1% of the time
where the time goes in v7:
time: 82 us; the launch traced here: 81.8 us
  Pallas kernels  81.2 us (99%)
    pallas_call x1, Pallas kernels, per_device(): pl.pallas_call(functools.partial(kernel, sizes), out_shape=(jax.ShapeDtyp...  78.9 us
    pallas_call x1, Pallas kernels, per_device(): pl.pallas_call(functools.partial(finish, math.sqrt(width * n_gene)), out_...  2.35 us

profile of v7, /device:TPU:1, one launch (start us, length us, event | category | flops | bytes accessed | tf_op | source)
XLA Modules:
  0.0 81.8 jit_solution(4558775806696516383)
XLA Ops:
  0.6 78.9 %lanczos.1 = (f32[5,32,32]{2,1,0:T(8,128)}, f32[32,4096]{1,0:T(8,128)}) custom-call(f32[1536,4096]{1,0:T(8,128)} %x_ref.1, s32[6,16]{1,0:T(8,128)} %mask_ref.1, f32[32,4096]{1,0:T(8,128)} %bitcast.2), custom_call_target="tpu_custom_call" | custom-call | tf_op jit(solution)/shard_map/lanczos/pallas_call | solution.py:526
  79.5 2.3 %finish.1 = (f32[2,32,32]{2,1,0:T(8,128)}, f32[2,32,32]{2,1,0:T(8,128)}, f32[32,4096]{1,0:T(8,128)}) custom-call(f32[5,32,32]{2,1,0:T(8,128)} %get-tuple-element.8.small_ref, f32[32,4096]{1,0:T(8,128)} %get-tuple-element.9.resid_ref), custom_call_target="tpu_custom_call" | custom-call | tf_op jit(solution)/shard_map/finish/pallas_call | solution.py:578

commit v8 on v7

--- a/solution.py
+++ b/solution.py
@@ -361,6 +361,21 @@
     for step in range(2):
         count = 2 + step
 
+        def to_side(step, stage, part, peer):
+            for d in range(1, SIDE):
+                pltpu.make_async_remote_copy(
+                    src_ref=part,
+                    dst_ref=part,
+                    send_sem=stat_send_sem.at[step, stage],
+                    recv_sem=stat_sem.at[step, stage],
+                    device_id=(peer(d), g),
+                    device_id_type=MESH,
+                ).start()
+
+        def take_stat(stage, tiles):
+            wait_bytes(stat_buf.at[step, stage, pl.ds(0, SIDE - 1), pl.ds(0, tiles)], stat_sem.at[step, stage])
+            return [sum_slots(stat_buf.at[step, stage, :, k], SIDE) for k in range(tiles)]
+
         def send_stat():
             if step == 0:
                 stat = dot(y3[0], y3[0], NT)
@@ -368,12 +383,12 @@
                 stat = dot(y3[1], jnp.concatenate([y3[1], y3[0]], axis=0), NT)
             row = fold_lanes(stat[3 * BLOCK : 3 * BLOCK + 8])
             stat = fold3(stat)
-            stat_buf[step, c, 0] = pack(fold_lanes(stat))
-            stat_buf[step, c, 1] = jnp.concatenate([row, jnp.zeros((8, 128 - BLOCK), F32)], axis=1)
+            mine = stat_buf.at[step, 0, x_at, pl.ds(0, count)]
+            mine[0] = pack(fold_lanes(stat))
+            mine[1] = jnp.concatenate([row, jnp.zeros((8, 128 - BLOCK), F32)], axis=1)
             if step == 1:
-                stat_buf[step, c, 2] = pack(fold_lanes(stat, with_ones))
-            here = stat_buf.at[step, c, pl.ds(0, count)]
-            to_cells(here, here, stat_send_sem.at[step], lambda k: stat_sem.at[step])
+                mine[2] = pack(fold_lanes(stat, with_ones))
+            to_side(step, 0, mine, lambda d: y_at * SIDE + lax.rem(x_at + d, SIDE))
 
         sent, got = i_send.at[step], i_recv.at[step]
 
@@ -409,6 +424,11 @@
 
             pl.when(t == 1)(send_stat)
 
+        for k, total in enumerate(take_stat(0, count)):
+            stat_buf[step, 1, y_at, k] = total
+        mine = stat_buf.at[step, 1, y_at, pl.ds(0, count)]
+        to_side(step, 1, mine, lambda d: lax.rem(y_at + d, SIDE) * SIDE + x_at)
+
         if step == 0:
             wait_bytes(column_recv.at[pl.ds(1, n_cell - 1)], column_sems.at[1])
             column_sums = column_part[:, own]
@@ -416,8 +436,7 @@
                 column_sums = column_sums + column_recv[k]
             column_sums = jnp.sum(column_sums, axis=0, keepdims=True)
 
-        wait_bytes(stat_buf.at[step, pl.ds(0, n_cell - 1), pl.ds(0, count)], stat_sem.at[step])
-        stats = [sum_slots(stat_buf.at[step, :, k], n_cell) / cells for k in range(count)]
+        stats = [total / cells for total in take_stat(1, count)]
         mean_row = stats[1][0:1, 0:BLOCK]
         mean_column = jnp.sum(jnp.where(eye, mean_row, 0.0), axis=1, keepdims=True)
         alpha = unpack(stats[0]) - mean_column * mean_row
@@ -491,7 +510,8 @@
                 for n in range(2):
                     wait_bytes(z_recv.at[k, n, pl.ds(1, n_gene - 1)], z_send_sem.at[k, n])
                     wait_bytes(z_recv.at[k, n, pl.ds(1, n_gene - 1)], zg_send_sem.at[k, n])
-                wait_bytes(stat_buf.at[k, pl.ds(0, n_cell - 1), pl.ds(0, 2 + k)], stat_send_sem.at[k])
+                for n in range(2):
+                    wait_bytes(stat_buf.at[k, n, pl.ds(0, SIDE - 1), pl.ds(0, 2 + k)], stat_send_sem.at[k, n])
                 wait_bytes(i_recv.at[k, pl.ds(1, n_cell - 1)], rs_send_sem.at[k])
             wait_bytes(resid.at[0, :, pl.ds(0, (n_cell - 1) * TILE)], ag_send_sem.at[0])
 
@@ -544,7 +564,7 @@
             pltpu.VMEM((2, BLOCK, rows), F32),
             pltpu.VMEM((2, 3 * BLOCK + 16, rows), BF16),
             pltpu.VMEM((2 * BLOCK, rows), FP8),
-            pltpu.VMEM((2, n_cell, 3, 8, 128), F32),
+            pltpu.VMEM((2, 2, SIDE, 3, 8, 128), F32),
             pltpu.VMEM((BLOCK, width), F32),
             pltpu.VMEM((2, n_cell, BLOCK, TILE), F32),
             pltpu.VMEM((2, n_cell, BLOCK, TILE), F32),
@@ -561,8 +581,8 @@
             dma((2, 2)),
             dma((2, 2)),
             dma((2, 2)),
-            dma((2,)),
-            dma((2,)),
+            dma((2, 2)),
+            dma((2, 2)),
             dma((2,)),
             dma((2,)),
             dma((2,)),

time: 82 us -> 80 us (0.976)
  Pallas kernels: 81.2 us -> 79.1 us
    pallas_call x1, Pallas kernels: 78.9 us -> 76.8 us  [per_device(): pl.pallas_call(functools.partial(kernel, sizes), out_shape=(jax.ShapeDtyp...]
where the time goes in v8:
time: 80 us; the launch traced here: 79.8 us
  Pallas kernels  79.1 us (99%)
    pallas_call x1, Pallas kernels, per_device(): pl.pallas_call(functools.partial(kernel, sizes), out_shape=(jax.ShapeDtyp...  76.8 us
    pallas_call x1, Pallas kernels, per_device(): pl.pallas_call(functools.partial(finish, math.sqrt(width * n_gene)), out_...  2.35 us

profile of v8, /device:TPU:1, one launch (start us, length us, event | category | flops | bytes accessed | tf_op | source)
XLA Modules:
  0.0 79.8 jit_solution(8783518056638448927)
XLA Ops:
  0.6 76.8 %lanczos.1 = (f32[5,32,32]{2,1,0:T(8,128)}, f32[32,4096]{1,0:T(8,128)}) custom-call(f32[1536,4096]{1,0:T(8,128)} %x_ref.1, s32[6,16]{1,0:T(8,128)} %mask_ref.1, f32[32,4096]{1,0:T(8,128)} %bitcast.2), custom_call_target="tpu_custom_call" | custom-call | tf_op jit(solution)/shard_map/lanczos/pallas_call | solution.py:546
  77.4 2.3 %finish.1 = (f32[2,32,32]{2,1,0:T(8,128)}, f32[2,32,32]{2,1,0:T(8,128)}, f32[32,4096]{1,0:T(8,128)}) custom-call(f32[5,32,32]{2,1,0:T(8,128)} %get-tuple-element.8.small_ref, f32[32,4096]{1,0:T(8,128)} %get-tuple-element.9.resid_ref), custom_call_target="tpu_custom_call" | custom-call | tf_op jit(solution)/shard_map/finish/pallas_call | solution.py:598

commit v9 on v8

--- a/solution.py
+++ b/solution.py
@@ -15,7 +15,7 @@
 BF16 = jnp.bfloat16
 FP8 = jnp.float8_e4m3fn
 LOW_SCALE = 4096.0
-PIVOTS = 8
+PIVOTS = 16
 GROUPS = ((0, 3), (3, 3))
 
 NN = ((1,), (0,))
@@ -422,7 +422,7 @@
             def _():
                 send_image(two, owner_two)
 
-            pl.when(t == 1)(send_stat)
+            pl.when(t == 0)(send_stat)
 
         for k, total in enumerate(take_stat(0, count)):
             stat_buf[step, 1, y_at, k] = total

time: 80 us -> 80.2 us (level)
  no operation moved by 1% of the time
where the time goes in v9:
time: 80.2 us; the launch traced here: 80 us
  Pallas kernels  79.3 us (99%)
    pallas_call x1, Pallas kernels, per_device(): pl.pallas_call(functools.partial(kernel, sizes), out_shape=(jax.ShapeDtyp...  77 us
    pallas_call x1, Pallas kernels, per_device(): pl.pallas_call(functools.partial(finish, math.sqrt(width * n_gene)), out_...  2.35 us

profile of v9, /device:TPU:1, one launch (start us, length us, event | category | flops | bytes accessed | tf_op | source)
XLA Modules:
  0.0 80.0 jit_solution(1488068452114514839)
XLA Ops:
  0.6 77.0 %lanczos.1 = (f32[5,32,32]{2,1,0:T(8,128)}, f32[32,4096]{1,0:T(8,128)}) custom-call(f32[1536,4096]{1,0:T(8,128)} %x_ref.1, s32[6,16]{1,0:T(8,128)} %mask_ref.1, f32[32,4096]{1,0:T(8,128)} %bitcast.2), custom_call_target="tpu_custom_call" | custom-call | tf_op jit(solution)/shard_map/lanczos/pallas_call | solution.py:546
  77.6 2.3 %finish.1 = (f32[2,32,32]{2,1,0:T(8,128)}, f32[2,32,32]{2,1,0:T(8,128)}, f32[32,4096]{1,0:T(8,128)}) custom-call(f32[5,32,32]{2,1,0:T(8,128)} %get-tuple-element.8.small_ref, f32[32,4096]{1,0:T(8,128)} %get-tuple-element.9.resid_ref), custom_call_target="tpu_custom_call" | custom-call | tf_op jit(solution)/shard_map/finish/pallas_call | solution.py:598
